TPU v7x, 256 devices: a whole 4x4x8 slice. The times are simulated.
256 devices in a mesh: replica: 32 (over z, x_lo, core), tensor: 8 (over x_hi, y).
Axes of the slice: x: 4 (x_hi: 2, x_lo: 2; x = x_hi * 2 + x_lo), y: 4, z: 8, core: 2. Of those that a mesh axis runs over, the one named last changes fastest.
Arguments:
- tokens: bfloat16 [32768, 8192], P('replica', 'tensor'), may hold values from -120 to 120
- norm_gain: float32 [8192], P('tensor'), may hold values from 0.5 to 1.5
- key_weight: bfloat16 [8192, 1024], P('tensor'), may hold values from -0.0625 to 0.0625
- key_cotangent: bfloat16 [32768, 1024], P('replica', 'tensor'), may hold values from -6 to 6
- local_delta: bfloat16 [32, 320, 8192], P('replica', 'tensor'), may hold values from -12 to 12
- outer_params: float32 [320, 8192], P('tensor'), may hold values from -0.75 to 0.75
- momentum: float32 [320, 8192], P('tensor'), may hold values from -3 to 3
Outputs:
- projected_keys: bfloat16 [32768, 1024], P('replica', 'tensor')
- token_grads: bfloat16 [32768, 8192], P('replica', 'tensor')
- row_projection: float32 [32768], P('replica')
- weight_grads: bfloat16 [32, 8192, 1024], P('replica', 'tensor')
- new_params: float32 [320, 8192], P('tensor')
- new_momentum: float32 [320, 8192], P('tensor')
All inputs are finite; a program needn't handle non-finite values.
Results may differ from a plain program's by a relative error of at most 0.017.
Values may be sent and summed in bfloat16 or wider, within the bound.
A program may use at most 128 MiB of HBM per device.

v0:
```python
import math

import jax
import jax.numpy as jnp
from jax import lax
from jax.sharding import PartitionSpec as P

SCALE_LOWEST = -7
SCALE_HIGHEST = 1
OUTER_RATE = 0.7
OUTER_MOMENTUM = 0.9
EPSILON = 1e-05
GRID_EDGES = (
    (0.25, 0.5, False),
    (0.75, 0.5, True),
    (1.25, 0.5, False),
    (1.75, 0.5, True),
    (2.5, 1.0, False),
    (3.5, 1.0, True),
    (5.0, 2.0, False),
)


def choose_scale(largest):
    scale_now = jnp.full(largest.shape, 2.0**SCALE_LOWEST, largest.dtype)
    for exponent in range(SCALE_LOWEST, SCALE_HIGHEST):
        scale_now = jnp.where(largest > 6.0 * 2.0**exponent, scale_now * 2.0, scale_now)
    return scale_now


def quantize_blocks(values):
    magnitude = jnp.abs(values)
    largest = jnp.max(magnitude, axis=-1)
    block_scale = choose_scale(largest).astype(jnp.bfloat16)
    scale_wide = block_scale.astype(jnp.float32)[..., None]
    levels = jnp.zeros_like(magnitude)
    for edge_value, step_size, upward in GRID_EDGES:
        threshold = edge_value * scale_wide
        passed = magnitude >= threshold if upward else magnitude > threshold
        levels = levels + jnp.where(passed, step_size, 0.0).astype(levels.dtype)
    block_code = jnp.where(values < 0, -levels, levels).astype(jnp.bfloat16)
    return (block_code, block_scale)


def expand_blocks(block_code, block_scale):
    return block_code.astype(jnp.float32) * block_scale.astype(jnp.float32)[..., None]


def per_device(tokens, norm_gain, key_weight, key_cotangent, local_delta, outer_params, momentum):
    tok_float = tokens.astype(jnp.float32)
    full_width = tokens.shape[1] * lax.axis_size("tensor")
    square_part = jnp.sum(tok_float * tok_float, axis=1)
    mean_square = lax.psum(square_part, "tensor") / full_width
    inv_rms = lax.rsqrt(mean_square + EPSILON)[:, None]
    unit_rows = tok_float * inv_rms
    normed = (unit_rows * norm_gain).astype(jnp.bfloat16)
    partial_value = jnp.dot(normed, key_weight, preferred_element_type=jnp.float32)
    projected_keys = lax.psum_scatter(
        partial_value.astype(jnp.bfloat16), "tensor", scatter_dimension=1, tiled=True
    )
    shard_piece = lax.all_gather(key_cotangent, "tensor", axis=1, tiled=True)
    d_normed = lax.dot_general(
        shard_piece, key_weight, (((1,), (1,)), ((), ())), preferred_element_type=jnp.float32
    )
    block_grad = lax.dot_general(
        normed, shard_piece, (((0,), (0,)), ((), ())), preferred_element_type=jnp.float32
    ).astype(jnp.bfloat16)
    grad_rows = block_grad
    d_normed, grad_rows = (d_normed, grad_rows)
    d_scaled = d_normed * norm_gain
    projected = lax.psum(jnp.sum(d_scaled * unit_rows, axis=1), "tensor") / full_width
    token_grads = (inv_rms * (d_scaled - unit_rows * projected[:, None])).astype(jnp.bfloat16)
    row_projection = projected * jnp.float32(math.sqrt(full_width))
    weight_grads = grad_rows[None]
    workers = lax.axis_size("replica")
    frag_rows, row_width = outer_params.shape
    blocks = frag_rows * row_width // (workers * 128)
    pseudo = local_delta.reshape(workers, blocks, 4, 32).astype(jnp.float32)
    block_codes, block_scales = quantize_blocks(pseudo)
    deq_terms = expand_blocks(block_codes, block_scales).reshape(workers, blocks, 128)
    own_sum = lax.psum_scatter(deq_terms, "replica", scatter_dimension=0, tiled=True).reshape(
        1, blocks, 4, 32
    )
    average = own_sum / workers
    average_codes, average_scales = quantize_blocks(average)
    all_codes, all_scales = (
        lax.all_gather(average_codes.reshape(1, blocks, 128), "replica", axis=0, tiled=True),
        lax.all_gather(average_scales, "replica", axis=0, tiled=True),
    )
    update = expand_blocks(all_codes.reshape(workers, blocks, 4, 32), all_scales).reshape(
        frag_rows, row_width
    )
    new_momentum = OUTER_MOMENTUM * momentum + update
    new_params = outer_params - OUTER_RATE * (update + OUTER_MOMENTUM * new_momentum)
    return (projected_keys, token_grads, row_projection, weight_grads, new_params, new_momentum)


def solution(mesh):
    placed = (
        P("replica", "tensor"),
        P("tensor"),
        P("tensor", None),
        P("replica", "tensor"),
        P("replica", "tensor", None),
        P("tensor", None),
        P("tensor", None),
    )
    return jax.shard_map(
        per_device,
        mesh=mesh,
        in_specs=placed,
        out_specs=(
            P("replica", "tensor"),
            P("replica", "tensor"),
            P("replica"),
            P("replica", "tensor", None),
            P("tensor", None),
            P("tensor", None),
        ),
        check_vma=False,
    )
```

profile of v0, /device:TPU:1, one launch (start us, length us, event | category | flops | bytes accessed | tf_op | source)
XLA Modules:
  0.0 333.2 jit_solution(4399358473763553728)
XLA Ops:
  9.4 5.0 %abs.35 = f32[32,80,4,32]{3,2,1,0:T(4,128)} reshape(f32[1,40,8192]{2,1,0:T(8,128)S(1)} %convert_abs_fusion) | data formatting | bytes 2621440 | tf_op jit(solution)/shard_map/abs | solution.py:32
  14.4 6.4 %reduce_max.18 = f32[32,80,4]{2,1,0:T(8,128)} reduce(f32[32,80,4,32]{3,2,1,0:T(4,128)} %abs.35, f32[]{:T(128)} %constant.31.clone.1), dimensions={3}, to_apply=%region_5.0 | reduce | flops 317440 | bytes 1351684 | tf_op jit(solution)/shard_map/reduce_max | solution.py:33
  20.8 1.7 copy.77
  24.6 2.0 convert_compare_fusion
  27.5 1.5 ge.72
  29.0 2.7 copy.88
  33.3 2.7 copy.90
  37.5 2.8 copy.92
  41.8 2.8 copy.94
  46.1 2.8 copy.96
  50.4 2.7 copy.98
  54.5 2.7 copy.100
  58.7 2.8 copy.86
  61.6 2.0 lt.23
  63.5 6.2 %convert_multiply_fusion.2 = f32[32,80,128]{2,1,0:T(8,128)} fusion(f32[32,80,128]{2,1,0:T(8,128)} %copy.100, pred[32,80,128]{2,1,0:T(8,128)(4,1)} %lt.23, f32[32,80,128]{2,1,0:T(8,128)S(1)} %copy-done.1, f32[32,80,128]{2,1,0:T(8,128)} %copy.98, f32[32,80,128]{2,1,0:T(8,128)} %copy.96, f32[32,80,128]{2,1,0:T(8,128)} %copy.94, f32[32,80,128]{2,1,0:T(8,128)} %copy.92, ...), kind=kLoop, calls=%fused_computation.19 | loop fusion | flops 8192000 | bytes 13434880 | tf_op jit(solution)/shard_map/mul | solution.py:46
  70.6 4.0 %copy.76 = bf16[1024,1024]{0,1:T(8,128)(2,1)} copy(bf16[1024,1024]{1,0:T(8,128)(2,1)} %param.7) | data formatting | bytes 4194304 | tf_op args[0]
  74.6 2.1 fusion.8
  76.7 21.7 %psum.14 = f32[1024]{0:T(1024)S(1)} all-reduce(f32[1024]{0:T(1024)S(1)} %fusion.8), channel_id=1, replica_groups=mesh['replica'=32,'tensor'=8] {'tensor'}, use_global_device_ids=true, to_apply=%region_1.0 | all-reduce | flops 1024 | bytes 8192 | tf_op jit(solution)/shard_map/psum | solution.py:53
  98.4 5.5 %convolution_convert_fusion = bf16[1024,1024]{1,0:T(8,128)(2,1)} fusion(bf16[1024,1024]{1,0:T(8,128)(2,1)S(1)} %copy-done, bf16[1024,1024]{0,1:T(8,128)(2,1)} %copy.76, f32[1024]{0:T(1024)S(1)} %copy-done.8, f32[1024]{0:T(1024)S(1)} %add_rsqrt_fusion), kind=kOutput, calls=%fused_computation.13 | convolution fusion | flops 2152726528 | bytes 6299648 | tf_op jit(solution)/shard_map/dot_general | solution.py:57
  103.9 4.0 %copy.112 = bf16[1024,1024]{0,1:T(8,128)(2,1)} copy(bf16[1024,1024]{1,0:T(8,128)(2,1)} %convolution_convert_fusion) | data formatting | bytes 4194304
  107.8 84.5 %reduce-scatter.5.cloned.1.call-done = f32[1,80,128]{2,1,0:T(8,128)} async-done(((f32[32,80,128]{2,1,0:T(8,128)}), f32[1,80,128]{2,1,0:T(8,128)}) %reduce-scatter.5.cloned.1.call-update) | async-done | bytes 40976 | tf_op jit(solution)/shard_map/reduce_scatter | solution.py:81
  194.8 36.3 %all_gather.10 = bf16[32,80,128]{2,1,0:T(8,128)(2,1)S(1)} all-gather(bf16[1,80,128]{2,1,0:T(8,128)(2,1)S(1)} %fusion.13), channel_id=1, replica_groups=mesh['replica'=32,'tensor'=8] {'replica'}, dimensions={0}, use_global_device_ids=true | all-gather | bytes 675840 | tf_op jit(solution)/shard_map/all_gather | solution.py:87
  232.4 32.4 %all_gather.11 = bf16[32,80,4]{1,2,0:T(4,128)(2,1)S(1)} all-gather(bf16[1,80,4]{1,2,0:T(4,128)(2,1)S(1)} %get-tuple-element.38), channel_id=1, replica_groups=mesh['replica'=32,'tensor'=8] {'replica'}, dimensions={0}, use_global_device_ids=true | all-gather | bytes 21120 | tf_op jit(solution)/shard_map/all_gather | solution.py:88
  265.3 5.0 %mul.799 = f32[32,80,4,32]{3,2,1,0:T(4,128)} broadcast(f32[32,80,4]{2,1,0:T(8,128)S(1)} %copy.110), dimensions={0,1,2} | broadcast | bytes 1351680 | tf_op jit(solution)/shard_map/mul | solution.py:46
  270.3 7.4 %mul.800 = f32[40,8192]{1,0:T(8,128)} reshape(f32[32,80,4,32]{3,2,1,0:T(4,128)} %mul.799) | data formatting | bytes 2621440 | tf_op jit(solution)/shard_map/mul | solution.py:46
  277.7 4.0 %multiply_subtract_fusion = (f32[40,8192]{1,0:T(8,128)}, f32[40,8192]{1,0:T(8,128)}) fusion(f32[40,8192]{1,0:T(8,128)} %param.12, f32[40,8192]{1,0:T(8,128)} %param.13, f32[40,8192]{1,0:T(8,128)S(1)} %copy-done.2, f32[40,8192]{1,0:T(8,128)} %mul.800), kind=kLoop, calls=%fused_computation.17 | loop fusion | flops 2293760 | bytes 7864320 | tf_op jit(solution)/shard_map/sub | solution.py:94
  281.7 6.6 %fusion.4 = (f32[1024]{0:T(1024)S(1)}, f32[1024,1024]{0,1:T(8,128)}) fusion(bf16[1024,1024]{0,1:T(8,128)(2,1)} %copy.76, f32[1024]{0:T(1024)S(1)} %copy-done.8, f32[1024]{0:T(1024)S(1)} %add_rsqrt_fusion, bf16[1024,1024]{1,0:T(8,128)(2,1)} %all-gather.2.cloned.1.call-done, bf16[1024,1024]{1,0:T(8,128)(2,1)S(1)} %copy-done), kind=kOutput, calls=%fused_computation.6 | convolution fusion | flops 2152725504 | bytes 10498048 | tf_op jit(solution)/shard_map/dot_general | solution.py:62
  288.3 20.2 %psum.15 = f32[1024]{0:T(1024)S(1)} all-reduce(f32[1024]{0:T(1024)S(1)} %get-tuple-element.65), channel_id=1, replica_groups=mesh['replica'=32,'tensor'=8] {'tensor'}, use_global_device_ids=true, to_apply=%region_4.0 | all-reduce | flops 1024 | bytes 8192 | tf_op jit(solution)/shard_map/psum | solution.py:71
  309.1 5.0 %fusion.7 = bf16[1024,1024]{0,1:T(8,128)(2,1)} fusion(bf16[1024,1024]{0,1:T(8,128)(2,1)} %copy.76, f32[1024,1024]{0,1:T(8,128)} %get-tuple-element.66, f32[1024]{0:T(1024)S(1)} %get-tuple-element.58, f32[1024]{0:T(1024)S(1)} %copy-done.8, f32[1024]{0:T(1024)S(1)} %add_rsqrt_fusion), kind=kLoop, calls=%fused_computation.9 | loop fusion | flops 7340032 | bytes 8400896 | tf_op jit(solution)/shard_map/convert_element_type | solution.py:72
  314.1 3.9 %copy.111 = bf16[1024,1024]{1,0:T(8,128)(2,1)} copy(bf16[1024,1024]{0,1:T(8,128)(2,1)} %fusion.7) | data formatting | bytes 4194304
  318.1 5.9 %convert_bitcast_fusion = bf16[1,1024,1024]{2,1,0:T(8,128)(2,1)} fusion(bf16[1024,1024]{1,0:T(8,128)(2,1)} %all-gather.2.cloned.1.call-done, bf16[1024,1024]{0,1:T(8,128)(2,1)} %copy.76, f32[1024]{0:T(1024)S(1)} %copy-done.8, f32[1024]{0:T(1024)S(1)} %add_rsqrt_fusion), kind=kOutput, calls=%fused_computation.11 | convolution fusion | flops 2152726528 | bytes 6299648 | tf_op jit(solution)/shard_map/dot_general | solution.py:65
  324.0 1.8 copy.113
  (71 shorter events, 20.4 us)
Async XLA Ops:
  8.0 90.4 %copy-start = (bf16[1024,1024]{1,0:T(8,128)(2,1)S(1)}, bf16[1024,1024]{1,0:T(8,128)(2,1)}, u32[]{:S(2)}) copy-start(bf16[1024,1024]{1,0:T(8,128)(2,1)} %param.9) | copy-start | bytes 6291460
  8.0 184.3 %reduce-scatter.5.cloned.1.call-start = ((), (), s32[]{:S(2)}) async-start(), calls=%async_computation.3 | async-start | bytes 1351680 | tf_op jit(solution)/shard_map/reduce_scatter | solution.py:81
  29.0 2.8 copy-start.7
  33.2 2.8 copy-start.6
  37.5 2.8 copy-start.5
  41.8 2.8 copy-start.4
  46.1 2.8 copy-start.3
  58.7 4.8 %copy-start.1 = (f32[32,80,128]{2,1,0:T(8,128)S(1)}, f32[32,80,128]{2,1,0:T(8,128)}, u32[]{:S(2)}) copy-start(f32[32,80,128]{2,1,0:T(8,128)} %abs.34) | copy-start | bytes 3932164
  69.8 211.9 %all-gather.2.cloned.1.call-start = ((), (), s32[]{:S(2)}) async-start(), calls=%async_computation.2 | async-start | bytes 2359296 | tf_op jit(solution)/shard_map/all_gather | solution.py:61
  70.4 253.6 %reduce-scatter.7.cloned.1.call-start = ((), (), s32[]{:S(2)}) async-start(), calls=%async_computation.4 | async-start | bytes 2359296
  74.6 23.8 %copy-start.8 = (f32[1024]{0:T(1024)S(1)}, f32[1024]{0:T(1024)}, u32[]{:S(2)}) copy-start(f32[1024]{0:T(1024)} %param.8) | copy-start | bytes 12292
  270.3 7.5 %copy-start.2 = (f32[40,8192]{1,0:T(8,128)S(1)}, f32[40,8192]{1,0:T(8,128)}, u32[]{:S(2)}) copy-start(f32[40,8192]{1,0:T(8,128)} %reshape.378) | copy-start | bytes 3932164
Sparse Core Ops, SparseCore 0:
  69.9 122.3 reduce-scatter.4
  196.9 81.9 reduce-scatter.6
Sparse Core Ops, SparseCore 1:
  73.0 63.1 all-gather.1
where the time goes:
time: 335 us; the launch traced here: 333 us
  blocking collectives  111 us (33%)
  waiting for transfers between devices  85.1 us (25%)
  local copies, waits for them, and re-layouts  73.4 us (22%)
  other arithmetic  30.2 us (9%)
  matrix products  18 us (5%)
  between operations  15.7 us (5%)
    reduce_scatter x1, waiting for transfers between devices, per_device(): lax.psum_scatter(deq_terms, 'replica', scatter_dimension=0, tiled=True)  84.5 us
    all_gather x1, blocking collectives, per_device(): lax.all_gather(average_codes.reshape(1, blocks, 128), 'replica', axis=0,...  36.3 us
    all_gather x1, blocking collectives, per_device(): lax.all_gather(average_scales, 'replica', axis=0, tiled=True)  32.4 us
    psum x1, blocking collectives, per_device(): mean_square = lax.psum(square_part, 'tensor') / full_width  21.7 us
    psum x1, blocking collectives, per_device(): lax.psum(jnp.sum(d_scaled * unit_rows, axis=1), 'tensor') / full_width  20.2 us
    gt x16, local copies, waits for them, and re-layouts, quantize_blocks(): passed = magnitude >= threshold if upward else magnitude > threshold  17.2 us
    mul x4, local copies, waits for them, and re-layouts, expand_blocks(): block_code.astype(jnp.float32) * block_scale.astype(jnp.float32)[..., None]  16.6 us
    unnamed x22, local copies, waits for them, and re-layouts  13.7 us
  transfers between devices with their start and end apart: 3, of which 1 were waited for; matrix products, arithmetic and copies ran while one was open for 17% of the time, Pallas kernels for 0%

commit v1 on v0

v1 whole, which is shorter than its diff:
```python
import functools
import math

import jax
import jax.numpy as jnp
from jax import lax
from jax.experimental import pallas as pl
from jax.experimental.pallas import tpu as pltpu
from jax.sharding import PartitionSpec as P

SCALE_LOWEST = -7
SCALE_HIGHEST = 1
OUTER_RATE = 0.7
OUTER_MOMENTUM = 0.9
EPSILON = 1e-05
GRID_EDGES = (
    (0.25, 0.5, False),
    (0.75, 0.5, True),
    (1.25, 0.5, False),
    (1.75, 0.5, True),
    (2.5, 1.0, False),
    (3.5, 1.0, True),
    (5.0, 2.0, False),
)
MESH = pl.DeviceIdType.MESH
LANES = 128
NX, NY = 4, 4
GROUP = 8
LOCAL = 4
N_REMOTE = 80
N_LOCAL = 16
F32 = jnp.float32
BF16 = jnp.bfloat16


def quantized(values, ones_blocks):
    magnitude = jnp.abs(values)
    weight = jnp.full(values.shape, 1.0, F32)
    for exponent in range(SCALE_LOWEST, SCALE_HIGHEST):
        weight = jnp.where(
            magnitude > 6.0 * 2.0**exponent, 64.0 ** (exponent - SCALE_LOWEST + 1), weight
        )
    total = jnp.dot(weight.astype(BF16), ones_blocks, preferred_element_type=F32)
    scale = jnp.full(values.shape, 2.0**SCALE_LOWEST, F32)
    back = jnp.full(values.shape, 2.0**-SCALE_LOWEST, F32)
    for exponent in range(SCALE_LOWEST, SCALE_HIGHEST):
        above = total >= 64.0 ** (exponent - SCALE_LOWEST + 1)
        scale = jnp.where(above, 2.0 ** (exponent + 1), scale)
        back = jnp.where(above, 2.0 ** -(exponent + 1), back)
    ratio = magnitude * back
    level = jnp.zeros(values.shape, F32)
    reached = 0.0
    for edge, step, upward in GRID_EDGES:
        reached += step
        passed = ratio >= edge if upward else ratio > edge
        level = jnp.where(passed, reached, level)
    level = level * scale
    return jnp.where(values < 0, -level, level)


def block_ones():
    row = lax.broadcasted_iota(jnp.int32, (LANES, LANES), 0) // 32
    column = lax.broadcasted_iota(jnp.int32, (LANES, LANES), 1) // 32
    return jnp.where(row == column, 1.0, 0.0).astype(BF16)


def kernel(
    full_width,
    tok_hbm,
    gain_ref,
    weight_hbm,
    cot_hbm,
    delta_ref,
    keys_hbm,
    tgrad_hbm,
    rowproj_ref,
    wgrad_hbm,
    update_ref,
    tok,
    wt,
    normed,
    normed_t,
    parts,
    cotg,
    dscaled,
    wgrad,
    tgrad,
    keys_out,
    inv_col,
    inv_row,
    other_row,
    sums,
    projs,
    x_relay,
    merge_in,
    merge_out,
    near,
    far_send,
    far_relay,
    far_in,
    qsend,
    r1,
    s1,
    r2,
    upd,
    ssem,
    rsem,
    lsem,
):
    r = lax.axis_index("replica")
    t = lax.axis_index("tensor")
    zs = lax.axis_size("replica") // LOCAL
    core = r % 2
    x_lo = (r // 2) % 2
    c = r % LOCAL
    z = r // LOCAL
    x_hi = t // NY
    y = t % NY
    x = x_hi * 2 + x_lo
    tokens_n, feats = tok.shape
    half = tokens_n // 2
    H = (pl.ds(0, half), pl.ds(half, half))
    yp, ym, y2 = (y + 1) % NY, (y + 3) % NY, (y + 2) % NY
    xp, xm = (x + 1) % NX, (x + 3) % NX

    def at_x(x_new):
        return ((z * 2 + x_new % 2) * 2 + core, (x_new // 2) * NY + y)

    dev_yp = (r, x_hi * NY + yp)
    dev_ym = (r, x_hi * NY + ym)
    dev_xp, dev_xm = at_x(xp), at_x(xm)
    dev_xlo = (z * LOCAL + (c + 2) % LOCAL, t)
    dev_core = (z * LOCAL + x_lo * 2 + (1 - core), t)
    c_xlo = (c + 2) % LOCAL
    c_core = x_lo * 2 + (1 - core)
    c_diag = (1 - x_lo) * 2 + (1 - core)
    t_far = (1 - x_hi) * NY + y

    names = {}
    pending = []

    def index_of(name):
        return names.setdefault(name, len(names))

    def send(name, src, dst, device):
        i = index_of(name)
        copy = pltpu.make_async_remote_copy(
            src_ref=src,
            dst_ref=dst,
            send_sem=ssem.at[i],
            recv_sem=rsem.at[i],
            device_id=device,
            device_id_type=MESH,
        )
        copy.start()
        pending.append(copy)

    def arrive(name, landing):
        i = index_of(name)
        pltpu.make_async_remote_copy(
            src_ref=landing,
            dst_ref=landing,
            send_sem=ssem.at[i],
            recv_sem=rsem.at[i],
            device_id=dev_yp,
            device_id_type=MESH,
        ).wait_recv()

    local = {}

    def fetch(name, src, dst):
        i = len(local)
        copy = pltpu.make_async_copy(src, dst, lsem.at[i])
        copy.start()
        local[name] = copy

    for h in range(2):
        fetch(("tok", h), tok_hbm.at[H[h]], tok.at[H[h]])
    fetch("weight", weight_hbm, wt)
    fetch("cot", cot_hbm, cotg.at[t])

    barrier = pltpu.get_barrier_semaphore()
    partners = [(r, (t + d) % GROUP) for d in range(1, GROUP)]
    partners += [(((z + d) % zs) * LOCAL + c, t) for d in range(1, zs)]
    partners += [dev_xp, dev_xm, dev_core, (z * LOCAL + c_diag, t)]
    for device in partners:
        pl.semaphore_signal(barrier, inc=1, device_id=device, device_id_type=MESH)
    pl.semaphore_wait(barrier, len(partners))

    send("x0", cot_hbm.at[H[0]], x_relay.at[0], dev_xp)
    send("x1", cot_hbm.at[H[1]], x_relay.at[1], dev_xm)
    send("own_p0", cot_hbm.at[H[0]], cotg.at[t, H[0]], dev_yp)
    send("own_m1", cot_hbm.at[H[1]], cotg.at[t, H[1]], dev_ym)
    send("own_p1", cot_hbm.at[H[1]], cotg.at[t, H[1]], dev_yp)
    send("own_m0", cot_hbm.at[H[0]], cotg.at[t, H[0]], dev_ym)

    blocks = tokens_n // LANES
    fblocks = feats // LANES

    def lane_sum_row(acc):
        return jnp.sum(acc.T, axis=0, keepdims=True)

    def column_of(row):
        return jnp.broadcast_to(row, (LANES, LANES)).T

    def sum_squares():
        @pl.loop(0, blocks // 2)
        def _(b):
            one(b)

        local[("tok", 1)].wait()

        @pl.loop(blocks // 2, blocks)
        def _(b):
            one(b)

    def one(b):
        rows = pl.ds(pl.multiple_of(b * LANES, LANES), LANES)
        acc = jnp.zeros((LANES, LANES), F32)
        for j in range(fblocks):
            v = tok[rows, j * LANES : (j + 1) * LANES].astype(F32)
            acc = acc + v * v
        sums[t, pl.ds(b, 1), :] = lane_sum_row(acc)

    local[("tok", 0)].wait()
    sum_squares()
    for d in range(1, GROUP):
        send(("sum", d), sums.at[t], sums.at[t], (r, (t + d) % GROUP))

    def relay_x():
        arrive("x0", x_relay.at[0])
        send("xf0", x_relay.at[0], cotg.at[(xm // 2) * NY + y, H[0]], dev_xp)
        arrive("x1", x_relay.at[1])
        send("xf1", x_relay.at[1], cotg.at[(xp // 2) * NY + y, H[1]], dev_xm)

    relay_x()

    share = delta_ref.shape[1] // (LOCAL * zs)
    frag = delta_ref.shape[0]
    width = share // LANES

    def quantize_share(s):
        ones_blocks = block_ones()
        pieces = [
            delta_ref[:, pl.ds(pl.multiple_of(s * share + k * LANES, LANES), LANES)].astype(F32)
            for k in range(width)
        ]
        values = jnp.concatenate(pieces, axis=0)
        qsend[s // zs, s % zs] = quantized(values, ones_blocks).astype(BF16)

    @pl.loop(0, LOCAL * zs)
    def _(s):
        quantize_share(s)

    for d in range(1, LOCAL):
        to = (c + d) % LOCAL
        send(("r1", d), qsend.at[to], r1.at[c], (z * LOCAL + to, t))

    t_ym, t_yp, t_y2 = x_hi * NY + ym, x_hi * NY + yp, x_hi * NY + y2
    f_ym, f_yp, f_y2 = ((1 - x_hi) * NY + k for k in (ym, yp, y2))
    arrive("own_p0", cotg.at[t_ym, H[0]])
    send("own_pp", cotg.at[t_ym, H[0]], cotg.at[t_ym, H[0]], dev_yp)
    arrive("own_m1", cotg.at[t_yp, H[1]])
    send("own_mm", cotg.at[t_yp, H[1]], cotg.at[t_yp, H[1]], dev_ym)

    for d in range(1, GROUP):
        arrive(("sum", d), sums.at[(t + GROUP - d) % GROUP])
    total = sums[0]
    for k in range(1, GROUP):
        total = total + sums[k]
    inv_row[...] = lax.rsqrt(total / full_width + EPSILON)

    @pl.loop(0, blocks)
    def _(b):
        rows = pl.ds(pl.multiple_of(b * LANES, LANES), LANES)
        column = column_of(inv_row[pl.ds(b, 1), :])
        inv_col[rows, :] = column
        for j in range(fblocks):
            cols = slice(j * LANES, (j + 1) * LANES)
            value = (tok[rows, cols].astype(F32) * column * gain_ref[:, cols]).astype(BF16)
            normed[rows, cols] = value
            normed_t[cols, rows] = value.T

    arrive("xf0", cotg.at[t_far, H[0]])
    send("far_p0", cotg.at[t_far, H[0]], cotg.at[t_far, H[0]], dev_yp)
    send("far_m0", cotg.at[t_far, H[0]], cotg.at[t_far, H[0]], dev_ym)
    arrive("xf1", cotg.at[t_far, H[1]])
    send("far_m1", cotg.at[t_far, H[1]], cotg.at[t_far, H[1]], dev_ym)
    send("far_p1", cotg.at[t_far, H[1]], cotg.at[t_far, H[1]], dev_yp)

    local["weight"].wait()

    @pl.loop(0, GROUP // 2)
    def _(n):
        cols = pl.ds(pl.multiple_of(n * 2 * LANES, LANES), 2 * LANES)
        for h in range(2):
            part = jnp.dot(normed[H[h], :], wt[:, cols], preferred_element_type=F32)
            parts[2 * n, H[h]] = part[:, :LANES].astype(BF16)
            parts[2 * n + 1, H[h]] = part[:, LANES:].astype(BF16)

    def target(s, y_new):
        return ((1 - x_hi) if s == 0 else x_hi) * NY + y_new

    for s in range(2):
        send(("d2p", s), parts.at[target(s, y2), H[0]], merge_in.at[s, 0], dev_yp)
        send(("d2m", s), parts.at[target(s, y2), H[1]], merge_in.at[s, 1], dev_ym)
        send(("d1p", s), parts.at[target(s, yp), H[1]], near.at[s, 0, H[1]], dev_yp)
        send(("d1m", s), parts.at[target(s, ym), H[0]], near.at[s, 1, H[0]], dev_ym)

    for d in range(1, LOCAL):
        arrive(("r1", d), r1.at[(c + LOCAL - d) % LOCAL])
    r1[c] = qsend[c]

    @pl.loop(0, zs)
    def _(k):
        s1[k] = (r1[0, k].astype(F32) + r1[1, k].astype(F32)) + (
            r1[2, k].astype(F32) + r1[3, k].astype(F32)
        )

    for d in range(1, zs):
        to = (z + d) % zs
        send(("r2", d), s1.at[to], r2.at[z], (to * LOCAL + c, t))
    r2[z] = s1[z]

    arrive("far_p0", cotg.at[f_ym, H[0]])
    send("far_pp", cotg.at[f_ym, H[0]], cotg.at[f_ym, H[0]], dev_yp)
    arrive("far_m1", cotg.at[f_yp, H[1]])
    send("far_mm", cotg.at[f_yp, H[1]], cotg.at[f_yp, H[1]], dev_ym)

    def weight_grad_pair(p):
        rhs = jnp.concatenate([cotg[2 * p], cotg[2 * p + 1]], axis=1)
        cols = pl.ds(pl.multiple_of(p * 2 * LANES, LANES), 2 * LANES)
        for h in range(2):
            rows = slice(h * (feats // 2), (h + 1) * (feats // 2))
            wgrad[rows, cols] = jnp.dot(
                normed_t[rows, :], rhs, preferred_element_type=F32
            ).astype(BF16)

    def weight_grad_side(x_side):
        @pl.loop(0, 2)
        def _(k):
            weight_grad_pair(x_side * 2 + k)

    local["cot"].wait()
    arrive("own_p1", cotg.at[t_ym, H[1]])
    arrive("own_m0", cotg.at[t_yp, H[0]])
    arrive("own_pp", cotg.at[t_y2, H[0]])
    arrive("own_mm", cotg.at[t_y2, H[1]])
    weight_grad_side(x_hi)

    def merge(s):
        arrive(("d2p", s), merge_in.at[s, 0])
        merge_out[s, 0] = (
            merge_in[s, 0].astype(F32) + parts[target(s, yp), H[0]].astype(F32)
        ).astype(BF16)
        send(("d1pp", s), merge_out.at[s, 0], near.at[s, 0, H[0]], dev_yp)
        arrive(("d2m", s), merge_in.at[s, 1])
        merge_out[s, 1] = (
            merge_in[s, 1].astype(F32) + parts[target(s, ym), H[1]].astype(F32)
        ).astype(BF16)
        send(("d1mm", s), merge_out.at[s, 1], near.at[s, 1, H[1]], dev_ym)

    merge(0)

    for d in range(1, zs):
        arrive(("r2", d), r2.at[(z + zs - d) % zs])
    total = r2[0]
    for k in range(1, zs):
        total = total + r2[k]
    upd[c, z] = quantized(total / (LOCAL * zs), block_ones()).astype(BF16)
    for d in range(1, zs):
        send(("r3", d), upd.at[c, z], upd.at[c, z], (((z + d) % zs) * LOCAL + c, t))

    merge(1)

    arrive("far_m0", cotg.at[f_yp, H[0]])
    arrive("far_p1", cotg.at[f_ym, H[1]])
    arrive("far_pp", cotg.at[f_y2, H[0]])
    arrive("far_mm", cotg.at[f_y2, H[1]])
    weight_grad_side(1 - x_hi)
    fetch("wgrad", wgrad, wgrad_hbm)

    for d in range(1, zs):
        arrive(("r3", d), upd.at[c, (z + zs - d) % zs])
    send("r4x", upd.at[c], upd.at[c], dev_xlo)
    send("r4c", upd.at[c], upd.at[c], dev_core)

    step = 2 * LANES if tokens_n % (2 * LANES) == 0 else LANES

    @pl.loop(0, tokens_n // step)
    def _(m):
        rows = pl.ds(pl.multiple_of(m * step, step), step)
        lhs = jnp.concatenate([cotg[k, rows, :] for k in range(GROUP)], axis=1)
        d = lax.dot_general(lhs, wt[...], (((1,), (1,)), ((), ())), preferred_element_type=F32)
        d = d * gain_ref[...]
        dscaled[rows, :] = d
        acc = jnp.zeros((step, LANES), F32)
        for j in range(fblocks):
            cols = slice(j * LANES, (j + 1) * LANES)
            acc = acc + d[:, cols] * tok[rows, cols].astype(F32)
        for k in range(step // LANES):
            projs[t, pl.ds(m * (step // LANES) + k, 1), :] = lane_sum_row(
                acc[k * LANES : (k + 1) * LANES]
            )

    for d in range(1, GROUP):
        send(("proj", d), projs.at[t], projs.at[t], (r, (t + d) % GROUP))

    def near_sum(s, h):
        own = parts[target(s, y), H[h]].astype(F32)
        return own + (near[s, 0, H[h]].astype(F32) + near[s, 1, H[h]].astype(F32))

    def near_arrive(s):
        arrive(("d1p", s), near.at[s, 0, H[1]])
        arrive(("d1m", s), near.at[s, 1, H[0]])
        arrive(("d1pp", s), near.at[s, 0, H[0]])
        arrive(("d1mm", s), near.at[s, 1, H[1]])

    near_arrive(0)
    far_send[H[0], :] = near_sum(0, 0).astype(BF16)
    send("k0", far_send.at[H[0]], far_relay.at[0], dev_xp)
    far_send[H[1], :] = near_sum(0, 1).astype(BF16)
    send("k1", far_send.at[H[1]], far_relay.at[1], dev_xm)

    arrive("r4x", upd.at[c_xlo])
    send("r4xc", upd.at[c_xlo], upd.at[c_xlo], dev_core)

    arrive("k0", far_relay.at[0])
    send("kf0", far_relay.at[0], far_in.at[H[0]], dev_xp)
    arrive("k1", far_relay.at[1])
    send("kf1", far_relay.at[1], far_in.at[H[1]], dev_xm)

    for d in range(1, GROUP):
        arrive(("proj", d), projs.at[(t + GROUP - d) % GROUP])
    total = projs[0]
    for k in range(1, GROUP):
        total = total + projs[k]
    projected = total * inv_row[...] / full_width
    rowproj_ref[...] = projected * math.sqrt(full_width)
    other_row[...] = projected * inv_row[...] * inv_row[...]

    @pl.loop(0, blocks)
    def _(b):
        rows = pl.ds(pl.multiple_of(b * LANES, LANES), LANES)
        column = inv_col[rows, :]
        other = column_of(other_row[pl.ds(b, 1), :])
        for j in range(fblocks):
            cols = slice(j * LANES, (j + 1) * LANES)
            tgrad[rows, cols] = (
                column * dscaled[rows, cols] - tok[rows, cols].astype(F32) * other
            ).astype(BF16)

    fetch("tgrad", tgrad, tgrad_hbm)

    arrive("r4c", upd.at[c_core])
    arrive("r4xc", upd.at[c_diag])

    @pl.loop(0, LOCAL * zs)
    def _(s):
        value = upd[s // zs, s % zs].astype(F32)
        for k in range(width):
            cols = pl.ds(pl.multiple_of(s * share + k * LANES, LANES), LANES)
            update_ref[:, cols] = value[k * frag : (k + 1) * frag, :]

    near_arrive(1)
    arrive("kf0", far_in.at[H[0]])
    keys_out[H[0], :] = (near_sum(1, 0) + far_in[H[0], :].astype(F32)).astype(BF16)
    arrive("kf1", far_in.at[H[1]])
    keys_out[H[1], :] = (near_sum(1, 1) + far_in[H[1], :].astype(F32)).astype(BF16)
    fetch("keys", keys_out, keys_hbm)

    for copy in pending:
        copy.wait_send()
    for name in ("wgrad", "tgrad", "keys"):
        local[name].wait()


def per_device(tokens, norm_gain, key_weight, key_cotangent, local_delta, outer_params, momentum):
    tok_n, feats = tokens.shape
    heads = key_weight.shape[1]
    full_width = feats * lax.axis_size("tensor")
    workers = lax.axis_size("replica")
    zs = workers // LOCAL
    frag, row_width = outer_params.shape
    share_rows = frag * row_width // workers // LANES
    half = tok_n // 2
    kb = key_cotangent.shape[1]
    any_spec = pl.BlockSpec(memory_space=pl.ANY)
    vmem = pl.BlockSpec(memory_space=pltpu.VMEM)
    blocks = tok_n // LANES
    keys, tgrad, rowproj, wgrad, update = pl.pallas_call(
        functools.partial(kernel, full_width),
        out_shape=(
            jax.ShapeDtypeStruct((tok_n, kb), BF16),
            jax.ShapeDtypeStruct((tok_n, feats), BF16),
            jax.ShapeDtypeStruct((blocks, LANES), F32),
            jax.ShapeDtypeStruct((feats, heads), BF16),
            jax.ShapeDtypeStruct((frag, row_width), F32),
        ),
        in_specs=[any_spec, vmem, any_spec, any_spec, vmem],
        out_specs=(any_spec, any_spec, vmem, any_spec, vmem),
        scratch_shapes=[
            pltpu.VMEM((tok_n, feats), BF16),
            pltpu.VMEM((feats, heads), BF16),
            pltpu.VMEM((tok_n, feats), BF16),
            pltpu.VMEM((feats, tok_n), BF16),
            pltpu.VMEM((GROUP, tok_n, kb), BF16),
            pltpu.VMEM((GROUP, tok_n, kb), BF16),
            pltpu.VMEM((tok_n, feats), F32),
            pltpu.VMEM((feats, heads), BF16),
            pltpu.VMEM((tok_n, feats), BF16),
            pltpu.VMEM((tok_n, kb), BF16),
            pltpu.VMEM((tok_n, LANES), F32),
            pltpu.VMEM((blocks, LANES), F32),
            pltpu.VMEM((blocks, LANES), F32),
            pltpu.VMEM((GROUP, blocks, LANES), F32),
            pltpu.VMEM((GROUP, blocks, LANES), F32),
            pltpu.VMEM((2, half, kb), BF16),
            pltpu.VMEM((2, 2, half, kb), BF16),
            pltpu.VMEM((2, 2, half, kb), BF16),
            pltpu.VMEM((2, 2, tok_n, kb), BF16),
            pltpu.VMEM((tok_n, kb), BF16),
            pltpu.VMEM((2, half, kb), BF16),
            pltpu.VMEM((tok_n, kb), BF16),
            pltpu.VMEM((LOCAL, zs, share_rows, LANES), BF16),
            pltpu.VMEM((LOCAL, zs, share_rows, LANES), BF16),
            pltpu.VMEM((zs, share_rows, LANES), F32),
            pltpu.VMEM((zs, share_rows, LANES), F32),
            pltpu.VMEM((LOCAL, zs, share_rows, LANES), BF16),
            pltpu.SemaphoreType.DMA((N_REMOTE,)),
            pltpu.SemaphoreType.DMA((N_REMOTE,)),
            pltpu.SemaphoreType.DMA((N_LOCAL,)),
        ],
        compiler_params=pltpu.CompilerParams(
            collective_id=0, has_side_effects=True, vmem_limit_bytes=44 * 1024 * 1024
        ),
        cost_estimate=pl.CostEstimate(
            flops=6 * tok_n * feats * heads, bytes_accessed=16 * 1024 * 1024, transcendentals=0
        ),
    )(tokens, norm_gain.reshape(1, feats), key_weight, key_cotangent, local_delta[0])
    new_momentum = OUTER_MOMENTUM * momentum + update
    new_params = outer_params - OUTER_RATE * (update + OUTER_MOMENTUM * new_momentum)
    return (keys, tgrad, rowproj.reshape(tok_n), wgrad[None], new_params, new_momentum)


def solution(mesh):
    placed = (
        P("replica", "tensor"),
        P("tensor"),
        P("tensor", None),
        P("replica", "tensor"),
        P("replica", "tensor", None),
        P("tensor", None),
        P("tensor", None),
    )
    return jax.shard_map(
        per_device,
        mesh=mesh,
        in_specs=placed,
        out_specs=(
            P("replica", "tensor"),
            P("replica", "tensor"),
            P("replica"),
            P("replica", "tensor", None),
            P("tensor", None),
            P("tensor", None),
        ),
        check_vma=False,
    )
```

time: 335 us -> 73.2 us (0.22)
  the two profiles are of different devices: /device:TPU:1 before, /device:TPU:4 now
where the time goes in v1:
time: 73.2 us; the launch traced here: 73 us
  Pallas kernels  62.3 us (85%)
  local copies, waits for them, and re-layouts  8.25 us (11%)
  other arithmetic  1.8 us (2%)
    pallas_call x1, Pallas kernels, per_device(): pl.pallas_call(functools.partial(kernel, full_width), out_shape=(jax.Shap...  62.3 us
    unnamed x16, local copies, waits for them, and re-layouts  8.25 us
    sub x1, other arithmetic, per_device(): outer_params - OUTER_RATE * (update + OUTER_MOMENTUM * new_momentum)  1.8 us

profile of v1, /device:TPU:4, one launch (start us, length us, event | category | flops | bytes accessed | tf_op | source)
XLA Modules:
  0.0 73.0 jit_solution(13648391344678022847)
XLA Ops:
  0.6 0.0 copy-start
  0.6 1.6 %copy-done = bf16[1024,1024]{1,0:T(8,128)(2,1)S(1)} copy-done((bf16[1024,1024]{1,0:T(8,128)(2,1)S(1)}, bf16[1024,1024]{1,0:T(8,128)(2,1)}, u32[]{:S(2)}) %copy-start) | copy-done | bytes 2097176
  2.2 0.0 copy-start.1
  2.2 1.1 %copy-done.1 = bf16[1,40,8192]{2,1,0:T(8,128)(2,1)S(1)} copy-done((bf16[1,40,8192]{2,1,0:T(8,128)(2,1)S(1)}, bf16[1,40,8192]{2,1,0:T(8,128)(2,1)}, u32[]{:S(2)}) %copy-start.1) | copy-done | bytes 655384
  3.3 0.0 copy-start.2
  3.3 0.9 %copy-done.2 = bf16[1024,128]{1,0:T(8,128)(2,1)S(1)} copy-done((bf16[1024,128]{1,0:T(8,128)(2,1)S(1)}, bf16[1024,128]{1,0:T(8,128)(2,1)}, u32[]{:S(2)}) %copy-start.2) | copy-done | bytes 262168
  4.3 0.0 copy-start.3
  4.3 0.7 copy-done.3
  5.0 0.0 copy-start.4
  5.0 0.0 copy-start.5
  5.0 62.3 %shard_map.118 = (bf16[1024,128]{1,0:T(8,128)(2,1)S(1)}, bf16[1024,1024]{1,0:T(8,128)(2,1)S(1)}, f32[8,128]{1,0:T(8,128)S(1)}, bf16[1024,1024]{1,0:T(8,128)(2,1)S(1)}, f32[40,8192]{1,0:T(8,128)S(1)}) custom-call(bf16[1024,1024]{1,0:T(8,128)(2,1)S(1)} %copy-done, f32[1,1024]{1,0:T(1,128)S(1)} %bitcast.7, bf16[1024,1024]{1,0:T(8,128)(2,1)} %weight_hbm.1, ...), custom_call_target="tpu_custom_call" | custom-call | flops 6442450944 | bytes 16777216 | tf_op jit(solution)/shard_map/pallas_call | solution.py:491
  67.2 0.0 copy-done.4
  67.2 0.0 copy-done.5
  67.2 1.8 %multiply_subtract_fusion = (f32[40,8192]{1,0:T(8,128)}, f32[40,8192]{1,0:T(8,128)}) fusion(f32[40,8192]{1,0:T(8,128)S(1)} %copy-done.4, f32[40,8192]{1,0:T(8,128)S(1)} %get-tuple-element.15, f32[40,8192]{1,0:T(8,128)S(1)} %copy-done.5), kind=kLoop, calls=%fused_computation | loop fusion | flops 1966080 | bytes 6553600 | tf_op jit(solution)/shard_map/sub | solution.py:542
  69.0 0.7 copy.17
  69.7 1.3 %copy.18 = bf16[1024,1024]{1,0:T(8,128)(2,1)} copy(bf16[1024,1024]{1,0:T(8,128)(2,1)S(1)} %get-tuple-element.25) | data formatting | bytes 4194304
  71.1 0.6 copy.19
  71.7 1.3 %copy.20 = bf16[1,1024,1024]{2,1,0:T(8,128)(2,1)} copy(bf16[1,1024,1024]{2,1,0:T(8,128)(2,1)S(1)} %bitcast.4) | data formatting | bytes 4194304
Async XLA Ops:
  0.6 1.6 %copy-start = (bf16[1024,1024]{1,0:T(8,128)(2,1)S(1)}, bf16[1024,1024]{1,0:T(8,128)(2,1)}, u32[]{:S(2)}) copy-start(bf16[1024,1024]{1,0:T(8,128)(2,1)} %tok_hbm.1) | copy-start | bytes 6291460
  2.2 1.1 %copy-start.1 = (bf16[1,40,8192]{2,1,0:T(8,128)(2,1)S(1)}, bf16[1,40,8192]{2,1,0:T(8,128)(2,1)}, u32[]{:S(2)}) copy-start(bf16[1,40,8192]{2,1,0:T(8,128)(2,1)} %param.11) | copy-start | bytes 1966084
  3.3 0.9 %copy-start.2 = (bf16[1024,128]{1,0:T(8,128)(2,1)S(1)}, bf16[1024,128]{1,0:T(8,128)(2,1)}, u32[]{:S(2)}) copy-start(bf16[1024,128]{1,0:T(8,128)(2,1)} %cot_hbm.1) | copy-start | bytes 786436
  4.3 0.7 copy-start.3
  5.0 62.3 %copy-start.4 = (f32[40,8192]{1,0:T(8,128)S(1)}, f32[40,8192]{1,0:T(8,128)}, u32[]{:S(2)}) copy-start(f32[40,8192]{1,0:T(8,128)} %param.12) | copy-start | bytes 3932164
  5.0 62.3 %copy-start.5 = (f32[40,8192]{1,0:T(8,128)S(1)}, f32[40,8192]{1,0:T(8,128)}, u32[]{:S(2)}) copy-start(f32[40,8192]{1,0:T(8,128)} %param.13) | copy-start | bytes 3932164

commit v2 on v0

v2 whole, which is shorter than its diff:
```python
import functools
import math

import jax
import jax.numpy as jnp
from jax import lax
from jax.experimental import pallas as pl
from jax.experimental.pallas import tpu as pltpu
from jax.sharding import PartitionSpec as P

SCALE_LOWEST = -7
SCALE_HIGHEST = 1
OUTER_RATE = 0.7
OUTER_MOMENTUM = 0.9
EPSILON = 1e-05
GRID_EDGES = (
    (0.25, 0.5, False),
    (0.75, 0.5, True),
    (1.25, 0.5, False),
    (1.75, 0.5, True),
    (2.5, 1.0, False),
    (3.5, 1.0, True),
    (5.0, 2.0, False),
)
MESH = pl.DeviceIdType.MESH
LANES = 128
NY = 4
GROUP = 8
LOCAL = 4
N_REMOTE = 96
N_LOCAL = 16
F32 = jnp.float32
BF16 = jnp.bfloat16


def quantized(values, ones_blocks):
    kind = values.dtype
    magnitude = jnp.abs(values)

    def const(value):
        return jnp.full(values.shape, value, kind)

    weight = const(1.0)
    for exponent in range(SCALE_LOWEST, SCALE_HIGHEST):
        weight = jnp.where(
            magnitude > const(6.0 * 2.0**exponent),
            const(64.0 ** (exponent - SCALE_LOWEST + 1)),
            weight,
        )
    total = jnp.dot(weight.astype(BF16), ones_blocks, preferred_element_type=F32).astype(kind)
    scale = const(2.0**SCALE_LOWEST)
    back = const(2.0**-SCALE_LOWEST)
    for exponent in range(SCALE_LOWEST, SCALE_HIGHEST):
        above = total >= const(64.0 ** (exponent - SCALE_LOWEST + 1))
        scale = jnp.where(above, const(2.0 ** (exponent + 1)), scale)
        back = jnp.where(above, const(2.0 ** -(exponent + 1)), back)
    ratio = magnitude * back
    level = const(0.0)
    reached = 0.0
    for edge, step, upward in GRID_EDGES:
        reached += step
        passed = ratio >= const(edge) if upward else ratio > const(edge)
        level = jnp.where(passed, const(reached), level)
    level = level * scale
    return jnp.where(values < const(0.0), -level, level)


def block_ones():
    row = lax.broadcasted_iota(jnp.int32, (LANES, LANES), 0) // 32
    column = lax.broadcasted_iota(jnp.int32, (LANES, LANES), 1) // 32
    return jnp.where(row == column, 1.0, 0.0).astype(BF16)


def kernel(
    full_width,
    tok_hbm,
    gain_hbm,
    weight_hbm,
    cot_hbm,
    delta_hbm,
    keys_ref,
    tgrad_ref,
    rowproj_ref,
    wgrad_ref,
    update_ref,
    tok,
    gain,
    delta,
    wt,
    scaled,
    normed_t,
    parts,
    cotg,
    dscaled,
    inv_col,
    inv_row,
    other_row,
    sums,
    projs,
    gin,
    xout,
    cin,
    two_out,
    merge_in,
    merge_out,
    near,
    qsend,
    r1,
    s1,
    r2,
    upd,
    ready,
    ssem,
    rsem,
    lsem,
):
    r = lax.axis_index("replica")
    t = lax.axis_index("tensor")
    zs = lax.axis_size("replica") // LOCAL
    core = r % 2
    x_lo = (r // 2) % 2
    z = r // LOCAL
    x_hi = t // NY
    y = t % NY
    tokens_n, feats = tok.shape
    half = tokens_n // 2
    H = (pl.ds(0, half), pl.ds(half, half))
    yp, ym, y2 = (y + 1) % NY, (y + 3) % NY, (y + 2) % NY
    e = core * 2 + x_lo
    e_xlo = core * 2 + (1 - x_lo)
    e_core = (1 - core) * 2 + x_lo
    e_diag = (1 - core) * 2 + (1 - x_lo)

    def of_local(z_new, e_new):
        return ((z_new * 2 + e_new % 2) * 2 + e_new // 2, t)

    dev_yp = (r, x_hi * NY + yp)
    dev_ym = (r, x_hi * NY + ym)
    ways = (dev_yp, dev_ym)
    t_far = (1 - x_hi) * NY + y
    dev_far = (r, t_far)

    names = {}
    pending = []

    def index_of(name):
        return names.setdefault(name, len(names))

    def send(name, src, dst, device):
        i = index_of(name)
        copy = pltpu.make_async_remote_copy(
            src_ref=src,
            dst_ref=dst,
            send_sem=ssem.at[i],
            recv_sem=rsem.at[i],
            device_id=device,
            device_id_type=MESH,
        )
        copy.start()
        pending.append(copy)

    def arrive(name, landing):
        i = index_of(name)
        pltpu.make_async_remote_copy(
            src_ref=landing,
            dst_ref=landing,
            send_sem=ssem.at[i],
            recv_sem=rsem.at[i],
            device_id=dev_yp,
            device_id_type=MESH,
        ).wait_recv()

    local = {}

    def fetch(name, src, dst):
        i = len(local)
        copy = pltpu.make_async_copy(src, dst, lsem.at[i])
        copy.start()
        local[name] = copy

    blocks = tokens_n // LANES
    fblocks = feats // LANES
    share = delta.shape[1] // (LOCAL * zs)
    frag = delta.shape[0]
    width = share // LANES
    t_ym, t_yp, t_y2 = x_hi * NY + ym, x_hi * NY + yp, x_hi * NY + y2
    f_ym, f_yp, f_y2 = ((1 - x_hi) * NY + k for k in (ym, yp, y2))

    def rows_of(b):
        return pl.ds(pl.multiple_of(b * LANES, LANES), LANES)

    def lane_sum_row(acc):
        return jnp.sum(acc.T, axis=0, keepdims=True)

    def column_of(row):
        return jnp.broadcast_to(row, (LANES, LANES)).T

    def load():
        fetch("delta", delta_hbm, delta)
        fetch("gain", gain_hbm, gain)
        for h in range(2):
            fetch(("tok", h), tok_hbm.at[H[h]], tok.at[H[h]])
        fetch("weight", weight_hbm, wt)
        fetch("cot", cot_hbm, cotg.at[t])

    def greet():
        barrier = pltpu.get_barrier_semaphore()

        def tell(device):
            pl.semaphore_signal(barrier, inc=1, device_id=device, device_id_type=MESH)

        for d in range(1, GROUP):
            tell((r - core, (t + d) % GROUP))
        tell(of_local(z, 1 - x_lo))

        @pl.when(core == 1)
        def _():
            tell(of_local(z, x_lo))

        for d in range(1, zs):
            tell(of_local((z + d) % zs, 2 + x_lo))

    def collect(collector, count, ready_sem):
        @pl.when(core == collector)
        def _():
            pl.semaphore_wait(pltpu.get_barrier_semaphore(), count)
            pl.semaphore_signal(
                ready_sem, inc=1, device_id=of_local(z, e_core), device_id_type=MESH
            )

        @pl.when(core != collector)
        def _():
            pl.semaphore_wait(ready_sem, 1)

    def meet():
        collect(0, 2 * GROUP + 1, ready.at[0])

    def meet_z():
        collect(1, 2 * (zs - 1), ready.at[1])

    def cot_start(i):
        h, k = H[i], H[1 - i]
        send(("own_p", i), cot_hbm.at[h], cotg.at[t, h], dev_yp)
        send(("own_m", 1 - i), cot_hbm.at[k], cotg.at[t, k], dev_ym)
        send(("c", i), cot_hbm.at[h], cotg.at[t, h], dev_far)

    def cot_onward(way):
        block = (t_ym, t_yp)[way]
        arrive((("own_p", "own_m")[way], way), cotg.at[block, H[way]])
        send(("own_on", way), cotg.at[block, H[way]], cotg.at[block, H[way]], ways[way])

    def cot_far_start(h):
        arrive(("c", h), cotg.at[t_far, H[h]])
        send(("far_p", h), cotg.at[t_far, H[h]], cotg.at[t_far, H[h]], dev_yp)
        send(("far_m", h), cotg.at[t_far, H[h]], cotg.at[t_far, H[h]], dev_ym)

    def cot_far_onward(way):
        block = (f_ym, f_yp)[way]
        arrive((("far_p", "far_m")[way], way), cotg.at[block, H[way]])
        send(("far_on", way), cotg.at[block, H[way]], cotg.at[block, H[way]], ways[way])

    def cot_own_end():
        local["cot"].wait()
        arrive(("own_p", 1), cotg.at[t_ym, H[1]])
        arrive(("own_m", 0), cotg.at[t_yp, H[0]])
        arrive(("own_on", 0), cotg.at[t_y2, H[0]])
        arrive(("own_on", 1), cotg.at[t_y2, H[1]])

    def cot_far_end():
        arrive(("far_m", 0), cotg.at[f_yp, H[0]])
        arrive(("far_p", 1), cotg.at[f_ym, H[1]])
        arrive(("far_on", 0), cotg.at[f_y2, H[0]])
        arrive(("far_on", 1), cotg.at[f_y2, H[1]])

    def sum_squares():
        def one(b):
            rows = rows_of(b)
            acc = jnp.zeros((LANES, LANES), F32)
            for j in range(fblocks):
                cols = slice(j * LANES, (j + 1) * LANES)
                v = tok[rows, cols].astype(F32)
                acc = acc + v * v
                scaled[rows, cols] = (v * gain[:, cols]).astype(BF16)
            sums[t, pl.ds(b, 1), :] = lane_sum_row(acc)

        local["gain"].wait()
        for h in range(2):
            local[("tok", h)].wait()
            pl.loop(h * blocks // 2, (h + 1) * blocks // 2)(one)

    def sum_squares_send():
        for d in range(1, GROUP):
            send(("sum", d), sums.at[t], sums.at[t], (r, (t + d) % GROUP))

    def sum_squares_end():
        for d in range(1, GROUP):
            arrive(("sum", d), sums.at[(t + GROUP - d) % GROUP])
        total = sums[0]
        for k in range(1, GROUP):
            total = total + sums[k]
        inv_row[...] = lax.rsqrt(total / full_width + EPSILON)

    def normed_rows():
        @pl.loop(0, blocks)
        def _(b):
            rows = rows_of(b)
            column = column_of(inv_row[pl.ds(b, 1), :])
            inv_col[rows, :] = column
            for j in range(fblocks):
                cols = slice(j * LANES, (j + 1) * LANES)
                value = (tok[rows, cols].astype(F32) * column * gain[:, cols]).astype(BF16)
                normed_t[cols, rows] = value.T

    def weight_ready():
        local["weight"].wait()

    def key_parts(x_side):
        @pl.loop(0, 2)
        def _(k):
            n = x_side * 2 + k
            cols = pl.ds(pl.multiple_of(n * 2 * LANES, LANES), 2 * LANES)
            for h in range(2):
                part = jnp.dot(scaled[H[h], :], wt[:, cols], preferred_element_type=F32)
                parts[2 * n, H[h]] = part[:, :LANES].astype(BF16)
                parts[2 * n + 1, H[h]] = part[:, LANES:].astype(BF16)

    def own_at(y_new):
        return x_hi * NY + y_new

    def far_at(y_new):
        return (1 - x_hi) * NY + y_new

    def plus(first, second):
        return (first.astype(F32) + second.astype(F32)).astype(BF16)

    def key_far_start(role):
        plus_block, minus_block = ((ym, yp), (yp, ym))[role]
        send(("g_p", role), parts.at[far_at(plus_block), H[1]], gin.at[role, 1], dev_yp)
        send(("g_m", role), parts.at[far_at(minus_block), H[0]], gin.at[role, 0], dev_ym)

    def key_cross(role, h):
        block = far_at((y2, y)[role])
        arrive((("g_m", "g_p")[h], role), gin.at[role, h])
        xout[role, h] = plus(gin[role, h], parts[block, H[h]])
        send(("x", role, h), xout.at[role, h], cin.at[role, h], dev_far)

    def key_own_start():
        send("d1p", parts.at[own_at(yp), H[1]], near.at[0, H[1]], dev_yp)
        send("d1m", parts.at[own_at(ym), H[0]], near.at[1, H[0]], dev_ym)

    def key_two_away(way):
        arrive(("x", 0, way), cin.at[0, way])
        two_out[way] = plus(cin[0, way], parts[own_at(y2), H[way]])
        send(("d2", way), two_out.at[way], merge_in.at[way], ways[way])

    def key_merge(way):
        arrive(("d2", way), merge_in.at[way])
        merge_out[way] = plus(merge_in[way], parts[own_at((yp, ym)[way]), H[way]])
        send(("d1", way), merge_out.at[way], near.at[way, H[way]], ways[way])

    def key_end():
        arrive("d1p", near.at[0, H[1]])
        arrive("d1m", near.at[1, H[0]])
        for h in range(2):
            arrive(("x", 1, h), cin.at[1, h])
        for h in range(2):
            arrive(("d1", h), near.at[h, H[h]])
            total = parts[own_at(y), H[h]].astype(F32) + cin[1, h].astype(F32)
            total = total + (near[0, H[h]].astype(F32) + near[1, H[h]].astype(F32))
            keys_ref[H[h], :] = (total * inv_col[H[h], :]).astype(BF16)

    def weight_grad_side(x_side):
        @pl.loop(0, 2)
        def _(k):
            p = x_side * 2 + k
            rhs = jnp.concatenate([cotg[2 * p], cotg[2 * p + 1]], axis=1)
            cols = pl.ds(pl.multiple_of(p * 2 * LANES, LANES), 2 * LANES)
            for h in range(2):
                rows = slice(h * (feats // 2), (h + 1) * (feats // 2))
                wgrad_ref[rows, cols] = jnp.dot(
                    normed_t[rows, :], rhs, preferred_element_type=F32
                ).astype(BF16)

    def normed_grads(first, last):
        step = 2 * LANES

        steps = tokens_n // step

        @pl.loop(first * steps // 4, last * steps // 4)
        def _(m):
            rows = pl.ds(pl.multiple_of(m * step, step), step)
            lhs = jnp.concatenate([cotg[k, rows, :] for k in range(GROUP)], axis=1)
            d = lax.dot_general(
                lhs, wt[...], (((1,), (1,)), ((), ())), preferred_element_type=F32
            )
            d = d * gain[...]
            dscaled[rows, :] = d
            acc = jnp.zeros((step, LANES), F32)
            for j in range(fblocks):
                cols = slice(j * LANES, (j + 1) * LANES)
                acc = acc + d[:, cols] * tok[rows, cols].astype(F32)
            for k in range(step // LANES):
                projs[t, pl.ds(m * (step // LANES) + k, 1), :] = lane_sum_row(
                    acc[k * LANES : (k + 1) * LANES]
                )

    def proj_send():
        for d in range(1, GROUP):
            send(("proj", d), projs.at[t], projs.at[t], (r, (t + d) % GROUP))

    def proj_end():
        for d in range(1, GROUP):
            arrive(("proj", d), projs.at[(t + GROUP - d) % GROUP])
        total = projs[0]
        for k in range(1, GROUP):
            total = total + projs[k]
        projected = total * inv_row[...] / full_width
        rowproj_ref[...] = projected * math.sqrt(full_width)
        other_row[...] = projected * inv_row[...] * inv_row[...]

    def token_grads():
        @pl.loop(0, blocks)
        def _(b):
            rows = rows_of(b)
            column = inv_col[rows, :]
            other = column_of(other_row[pl.ds(b, 1), :])
            for j in range(fblocks):
                cols = slice(j * LANES, (j + 1) * LANES)
                tgrad_ref[rows, cols] = (
                    column * dscaled[rows, cols] - tok[rows, cols].astype(F32) * other
                ).astype(BF16)

    def quantize(first, last):
        if first == 0:
            local["delta"].wait()
        ones_blocks = block_ones()

        @pl.loop(first * zs // 2, last * zs // 2)
        def _(i):
            shares = (2 * i, 2 * i + 1)
            pieces = [
                delta[:, pl.ds(pl.multiple_of(s * share + k * LANES, LANES), LANES)]
                for s in shares
                for k in range(width)
            ]
            values = jnp.concatenate([v.astype(F32) for v in pieces], axis=0).astype(BF16)
            coded = quantized(values, ones_blocks)
            for n, s in enumerate(shares):
                qsend[s % LOCAL, s // LOCAL] = coded[n * width * frag : (n + 1) * width * frag]

    share_rows = qsend.shape[2]
    cut = share_rows // 32 * 16
    pieces = (slice(0, share_rows - cut), slice(share_rows - cut, share_rows))
    far_first = sorted(range(1, zs), key=lambda d: -min(d, zs - d))

    def delta_start(i):
        p = pieces[i]
        for d in (2, 1, 3):
            to = (e + d) % LOCAL
            send(("r1", i, d), qsend.at[to, :, p], r1.at[e, :, p], of_local(z, to))

    def delta_sum(i):
        p = pieces[i]
        r1[e, :, p, :] = qsend[e, :, p, :]
        for d in range(1, LOCAL):
            arrive(("r1", i, d), r1.at[(e + LOCAL - d) % LOCAL, :, p])

        @pl.loop(0, zs)
        def _(k):
            s1[k, p, :] = (r1[0, k, p, :].astype(F32) + r1[1, k, p, :].astype(F32)) + (
                r1[2, k, p, :].astype(F32) + r1[3, k, p, :].astype(F32)
            )

        r2[z, p, :] = s1[z, p, :]

    def delta_z(i):
        p = pieces[i]
        for d in far_first:
            to = (z + d) % zs
            send(("r2", i, d), s1.at[to, p], r2.at[z, p], of_local(to, e))

    def delta_average(i):
        p = pieces[i]
        for d in range(1, zs):
            arrive(("r2", i, d), r2.at[(z + zs - d) % zs, p])
        total = r2[0, p, :]
        for k in range(1, zs):
            total = total + r2[k, p, :]
        upd[e, z, p, :] = quantized(total / (LOCAL * zs), block_ones()).astype(BF16)
        for d in far_first:
            send(("r3", i, d), upd.at[e, z, p], upd.at[e, z, p], of_local((z + d) % zs, e))

    def update_local(i):
        p = pieces[i]
        for d in range(1, zs):
            arrive(("r3", i, d), upd.at[e, (z + zs - d) % zs, p])
        send(("r4x", i), upd.at[e, :, p], upd.at[e, :, p], of_local(z, e_xlo))
        send(("r4c", i), upd.at[e, :, p], upd.at[e, :, p], of_local(z, e_core))

    def update_core(i):
        p = pieces[i]
        arrive(("r4x", i), upd.at[e_xlo, :, p])
        send(("r4xc", i), upd.at[e_xlo, :, p], upd.at[e_xlo, :, p], of_local(z, e_core))

    def update_end():
        for i, p in enumerate(pieces):
            arrive(("r4c", i), upd.at[e_core, :, p])
            arrive(("r4xc", i), upd.at[e_diag, :, p])

        @pl.loop(0, LOCAL * zs)
        def _(s):
            value = upd[s % LOCAL, s // LOCAL].astype(F32)
            for k in range(width):
                cols = pl.ds(pl.multiple_of(s * share + k * LANES, LANES), LANES)
                update_ref[:, cols] = value[k * frag : (k + 1) * frag, :]

    load()
    greet()
    quantize(0, 4)
    meet()
    delta_start(0)
    cot_start(0)
    cot_start(1)
    delta_start(1)
    sum_squares()
    weight_ready()
    key_parts(1 - x_hi)
    key_far_start(0)
    sum_squares_send()
    cot_onward(0)
    cot_onward(1)
    cot_far_start(0)
    delta_sum(0)
    meet_z()
    delta_z(0)
    key_cross(0, 0)
    key_cross(0, 1)
    key_far_start(1)
    delta_sum(1)
    delta_z(1)
    sum_squares_end()
    normed_rows()
    key_parts(x_hi)
    cot_far_start(1)
    cot_own_end()
    key_two_away(0)
    key_two_away(1)
    delta_average(0)
    key_cross(1, 0)
    cot_far_onward(0)
    key_cross(1, 1)
    cot_far_onward(1)
    delta_average(1)
    key_merge(0)
    key_merge(1)
    key_own_start()
    weight_grad_side(x_hi)
    update_local(0)
    cot_far_end()
    normed_grads(0, 4)
    proj_send()
    update_local(1)
    weight_grad_side(1 - x_hi)
    update_core(0)
    update_core(1)
    key_end()
    proj_end()
    token_grads()
    update_end()

    for copy in pending:
        copy.wait_send()


def finish_kernel(
    keys_ref,
    tgrad_ref,
    rowproj_ref,
    wgrad_ref,
    update_ref,
    params_ref,
    momentum_ref,
    keys_hbm,
    tgrad_hbm,
    rowproj_hbm,
    wgrad_hbm,
    params_hbm,
    momentum_hbm,
    new_params,
    new_momentum,
    sem,
):
    moves = [
        (wgrad_ref, wgrad_hbm),
        (tgrad_ref, tgrad_hbm),
        (keys_ref, keys_hbm),
        (rowproj_ref, rowproj_hbm),
    ]
    copies = [pltpu.make_async_copy(a, b, sem.at[i]) for i, (a, b) in enumerate(moves)]
    for copy in copies:
        copy.start()
    rows, columns = new_params.shape
    parts = 4
    step = columns // parts
    for k in range(parts):
        cols = pl.ds(k * step, step)

        @pl.loop(0, rows // 8)
        def _(b):
            at = (pl.ds(pl.multiple_of(b * 8, 8), 8), cols)
            update = update_ref[at]
            moved = OUTER_MOMENTUM * momentum_ref[at] + update
            new_momentum[at] = moved
            new_params[at] = params_ref[at] - OUTER_RATE * (update + OUTER_MOMENTUM * moved)

        for j, (a, b) in enumerate(((new_params, params_hbm), (new_momentum, momentum_hbm))):
            copy = pltpu.make_async_copy(
                a.at[:, cols], b.at[:, cols], sem.at[len(moves) + 2 * k + j]
            )
            copy.start()
            copies.append(copy)
    for copy in copies:
        copy.wait()


def per_device(tokens, norm_gain, key_weight, key_cotangent, local_delta, outer_params, momentum):
    tok_n, feats = tokens.shape
    heads = key_weight.shape[1]
    full_width = feats * lax.axis_size("tensor")
    workers = lax.axis_size("replica")
    zs = workers // LOCAL
    frag, row_width = outer_params.shape
    share_rows = frag * row_width // workers // LANES
    half = tok_n // 2
    kb = key_cotangent.shape[1]
    hbm = pl.BlockSpec(memory_space=pltpu.HBM)
    vmem = pl.BlockSpec(memory_space=pltpu.VMEM)
    blocks = tok_n // LANES
    operands = (tokens, norm_gain.reshape(1, feats), key_weight, key_cotangent, local_delta[0])
    keys, tgrad, rowproj, wgrad, update = pl.pallas_call(
        functools.partial(kernel, full_width),
        out_shape=(
            jax.ShapeDtypeStruct((tok_n, kb), BF16),
            jax.ShapeDtypeStruct((tok_n, feats), BF16),
            jax.ShapeDtypeStruct((blocks, LANES), F32),
            jax.ShapeDtypeStruct((feats, heads), BF16),
            jax.ShapeDtypeStruct((frag, row_width), F32),
        ),
        in_specs=[hbm] * 5,
        out_specs=(vmem,) * 5,
        scratch_shapes=[
            pltpu.VMEM((tok_n, feats), BF16),
            pltpu.VMEM((1, feats), F32),
            pltpu.VMEM(local_delta.shape[1:], BF16),
            pltpu.VMEM((feats, heads), BF16),
            pltpu.VMEM((tok_n, feats), BF16),
            pltpu.VMEM((feats, tok_n), BF16),
            pltpu.VMEM((GROUP, tok_n, kb), BF16),
            pltpu.VMEM((GROUP, tok_n, kb), BF16),
            pltpu.VMEM((tok_n, feats), F32),
            pltpu.VMEM((tok_n, LANES), F32),
            pltpu.VMEM((blocks, LANES), F32),
            pltpu.VMEM((blocks, LANES), F32),
            pltpu.VMEM((GROUP, blocks, LANES), F32),
            pltpu.VMEM((GROUP, blocks, LANES), F32),
            pltpu.VMEM((2, 2, half, kb), BF16),
            pltpu.VMEM((2, 2, half, kb), BF16),
            pltpu.VMEM((2, 2, half, kb), BF16),
            pltpu.VMEM((2, half, kb), BF16),
            pltpu.VMEM((2, half, kb), BF16),
            pltpu.VMEM((2, half, kb), BF16),
            pltpu.VMEM((2, tok_n, kb), BF16),
            pltpu.VMEM((LOCAL, zs, share_rows, LANES), BF16),
            pltpu.VMEM((LOCAL, zs, share_rows, LANES), BF16),
            pltpu.VMEM((zs, share_rows, LANES), F32),
            pltpu.VMEM((zs, share_rows, LANES), F32),
            pltpu.VMEM((LOCAL, zs, share_rows, LANES), BF16),
            pltpu.SemaphoreType.REGULAR((2,)),
            pltpu.SemaphoreType.DMA((N_REMOTE,)),
            pltpu.SemaphoreType.DMA((N_REMOTE,)),
            pltpu.SemaphoreType.DMA((N_LOCAL,)),
        ],
        compiler_params=pltpu.CompilerParams(
            collective_id=0, has_side_effects=True, vmem_limit_bytes=44 * 1024 * 1024
        ),
        cost_estimate=pl.CostEstimate(
            flops=6 * tok_n * feats * heads, bytes_accessed=16 * 1024 * 1024, transcendentals=0
        ),
    )(*(pltpu.with_memory_space_constraint(a, pltpu.HBM) for a in operands))
    keys, tgrad, rowproj, wgrad, new_params, new_momentum = pl.pallas_call(
        finish_kernel,
        out_shape=(
            jax.ShapeDtypeStruct((tok_n, kb), BF16),
            jax.ShapeDtypeStruct((tok_n, feats), BF16),
            jax.ShapeDtypeStruct((blocks, LANES), F32),
            jax.ShapeDtypeStruct((feats, heads), BF16),
            jax.ShapeDtypeStruct((frag, row_width), F32),
            jax.ShapeDtypeStruct((frag, row_width), F32),
        ),
        in_specs=[vmem] * 7,
        out_specs=(hbm,) * 6,
        scratch_shapes=[
            pltpu.VMEM((frag, row_width), F32),
            pltpu.VMEM((frag, row_width), F32),
            pltpu.SemaphoreType.DMA((12,)),
        ],
        compiler_params=pltpu.CompilerParams(vmem_limit_bytes=16 * 1024 * 1024),
        cost_estimate=pl.CostEstimate(
            flops=8 * frag * row_width, bytes_accessed=8 * 1024 * 1024, transcendentals=0
        ),
    )(keys, tgrad, rowproj, wgrad, update, outer_params, momentum)
    return (keys, tgrad, rowproj.reshape(tok_n), wgrad[None], new_params, new_momentum)


def solution(mesh):
    placed = (
        P("replica", "tensor"),
        P("tensor"),
        P("tensor", None),
        P("replica", "tensor"),
        P("replica", "tensor", None),
        P("tensor", None),
        P("tensor", None),
    )
    return jax.shard_map(
        per_device,
        mesh=mesh,
        in_specs=placed,
        out_specs=(
            P("replica", "tensor"),
            P("replica", "tensor"),
            P("replica"),
            P("replica", "tensor", None),
            P("tensor", None),
            P("tensor", None),
        ),
        check_vma=False,
    )
```

time: 335 us -> 54.4 us (0.16)
  blocking collectives: 111 us -> 0 us
  waiting for transfers between devices: 85.1 us -> 0 us
  local copies, waits for them, and re-layouts: 73.4 us -> 0.01 us
  Pallas kernels: 0 us -> 53.6 us
  other arithmetic: 30.2 us -> 0 us
  matrix products: 18 us -> 0 us
  between operations: 15.7 us -> 0.67 us
    reduce_scatter x1 -> x0, waiting for transfers between devices: 84.5 us -> none  [per_device(): lax.psum_scatter(deq_terms, 'replica', scatter_dimension=0, tiled=True)]
    all_gather x2 -> x0, blocking collectives: 68.7 us -> none  [the longest x1 36.3 us: per_device(): lax.all_gather(average_codes.reshape(1, blocks, 128), 'replica', axis=0,...]
    pallas_call x0 -> x2, Pallas kernels: none -> 53.6 us  [the longest x1 50.6 us: per_device(): pl.pallas_call(functools.partial(kernel, full_width), out_shape=(jax.Shap...]
    psum x2 -> x0, blocking collectives: 41.9 us -> none  [the longest x1 21.7 us: per_device(): mean_square = lax.psum(square_part, 'tensor') / full_width]
    dot_general x3 -> x0, matrix products: 18 us -> none  [the longest x1 6.57 us: per_device(): lax.dot_general(shard_piece, key_weight, (((1,), (1,)), ((), ())), prefer...]
    mul x11 -> x0, local copies, waits for them, and re-layouts: 17.7 us -> none  [the longest x4 16.6 us: expand_blocks(): block_code.astype(jnp.float32) * block_scale.astype(jnp.float32)[..., None]]
    gt x16 -> x0, local copies, waits for them, and re-layouts: 17.2 us -> none  [quantize_blocks(): passed = magnitude >= threshold if upward else magnitude > threshold]
    unnamed x22 -> x4, local copies, waits for them, and re-layouts: 13.7 us -> 0.01 us
  transfers between devices with their start and end apart: 3 -> 0, of which waited for: 1 -> 0; matrix products, arithmetic and copies ran while one was open for 17% -> 0% of each run, Pallas kernels for 0% -> 0%
where the time goes in v2:
time: 54.4 us; the launch traced here: 54.3 us
  Pallas kernels  53.6 us (99%)
  between operations  0.67 us (1%)
    pallas_call x1, Pallas kernels, per_device(): pl.pallas_call(functools.partial(kernel, full_width), out_shape=(jax.Shap...  50.6 us
    pallas_call x1, Pallas kernels, per_device(): pl.pallas_call(finish_kernel, out_shape=(jax.ShapeDtypeStruct((tok_n, kb)...  2.99 us

profile of v2, /device:TPU:1, one launch (start us, length us, event | category | flops | bytes accessed | tf_op | source)
XLA Modules:
  0.0 54.3 jit_solution(6734121505795712219)
XLA Ops:
  0.6 0.0 copy-start
  0.6 0.0 copy-start.1
  0.7 50.6 %shard_map.118 = (bf16[1024,128]{1,0:T(8,128)(2,1)S(1)}, bf16[1024,1024]{1,0:T(8,128)(2,1)S(1)}, f32[8,128]{1,0:T(8,128)S(1)}, bf16[1024,1024]{1,0:T(8,128)(2,1)S(1)}, f32[40,8192]{1,0:T(8,128)S(1)}) custom-call(bf16[1024,1024]{1,0:T(8,128)(2,1)} %tok_hbm.1, f32[1,1024]{1,0:T(1,128)} %bitcast.6, bf16[1024,1024]{1,0:T(8,128)(2,1)} %weight_hbm.1, ...), custom_call_target="tpu_custom_call" | custom-call | flops 6442450944 | bytes 16777216 | tf_op jit(solution)/shard_map/pallas_call | solution.py:640
  51.3 0.0 copy-done
  51.3 0.0 copy-done.1
  51.3 3.0 %shard_map.119 = (bf16[1024,128]{1,0:T(8,128)(2,1)}, bf16[1024,1024]{1,0:T(8,128)(2,1)}, f32[8,128]{1,0:T(8,128)}, bf16[1024,1024]{1,0:T(8,128)(2,1)}, f32[40,8192]{1,0:T(8,128)}, /*index=5*/f32[40,8192]{1,0:T(8,128)}) custom-call(bf16[1024,128]{1,0:T(8,128)(2,1)S(1)} %get-tuple-element.17.keys_ref, bf16[1024,1024]{1,0:T(8,128)(2,1)S(1)} %get-tuple-element.18.tgrad_ref, ...), custom_call_target="tpu_custom_call" | custom-call | flops 2621440 | bytes 8388608 | tf_op jit(solution)/shard_map/pallas_call | solution.py:690
Async XLA Ops:
  0.6 50.6 %copy-start = (f32[40,8192]{1,0:T(8,128)S(1)}, f32[40,8192]{1,0:T(8,128)}, u32[]{:S(2)}) copy-start(f32[40,8192]{1,0:T(8,128)} %params_ref.1) | copy-start | bytes 3932164
  0.6 50.6 %copy-start.1 = (f32[40,8192]{1,0:T(8,128)S(1)}, f32[40,8192]{1,0:T(8,128)}, u32[]{:S(2)}) copy-start(f32[40,8192]{1,0:T(8,128)} %momentum_ref.1) | copy-start | bytes 3932164

commit v3 on v2

--- a/solution.py
+++ b/solution.py
@@ -27,7 +27,7 @@
 NY = 4
 GROUP = 8
 LOCAL = 4
-N_REMOTE = 96
+N_REMOTE = 112
 N_LOCAL = 16
 F32 = jnp.float32
 BF16 = jnp.bfloat16
@@ -65,6 +65,17 @@
     return jnp.where(values < const(0.0), -level, level)
 
 
+def weight_grad_pair(pair, cotg, normed_t, out):
+    rhs = jnp.concatenate([cotg[2 * pair], cotg[2 * pair + 1]], axis=1)
+    cols = pl.ds(pl.multiple_of(pair * 2 * LANES, LANES), 2 * LANES)
+    feats = normed_t.shape[0]
+    for h in range(2):
+        rows = slice(h * (feats // 2), (h + 1) * (feats // 2))
+        out[rows, cols] = jnp.dot(
+            normed_t[rows, :], rhs, preferred_element_type=F32
+        ).astype(BF16)
+
+
 def block_ones():
     row = lax.broadcasted_iota(jnp.int32, (LANES, LANES), 0) // 32
     column = lax.broadcasted_iota(jnp.int32, (LANES, LANES), 1) // 32
@@ -82,21 +93,22 @@
     tgrad_ref,
     rowproj_ref,
     wgrad_ref,
-    update_ref,
+    upd,
+    cotg,
+    normed_t,
     tok,
     gain,
     delta,
     wt,
     scaled,
-    normed_t,
     parts,
-    cotg,
-    dscaled,
+    dpart,
     inv_col,
     inv_row,
     other_row,
     sums,
     projs,
+    half_proj,
     gin,
     xout,
     cin,
@@ -108,7 +120,6 @@
     r1,
     s1,
     r2,
-    upd,
     ready,
     ssem,
     rsem,
@@ -203,12 +214,14 @@
         fetch("weight", weight_hbm, wt)
         fetch("cot", cot_hbm, cotg.at[t])
 
+    far_first = sorted(range(1, zs), key=lambda d: -min(d, zs - d))
+
+    def tell(device):
+        pl.semaphore_signal(
+            pltpu.get_barrier_semaphore(), inc=1, device_id=device, device_id_type=MESH
+        )
+
     def greet():
-        barrier = pltpu.get_barrier_semaphore()
-
-        def tell(device):
-            pl.semaphore_signal(barrier, inc=1, device_id=device, device_id_type=MESH)
-
         for d in range(1, GROUP):
             tell((r - core, (t + d) % GROUP))
         tell(of_local(z, 1 - x_lo))
@@ -217,8 +230,10 @@
         def _():
             tell(of_local(z, x_lo))
 
-        for d in range(1, zs):
-            tell(of_local((z + d) % zs, 2 + x_lo))
+    def greet_z():
+        for d in far_first:
+            tell(of_local((z + d) % zs, 2))
+            tell(of_local((z + d) % zs, 3))
 
     def collect(collector, count, ready_sem):
         @pl.when(core == collector)
@@ -236,7 +251,7 @@
         collect(0, 2 * GROUP + 1, ready.at[0])
 
     def meet_z():
-        collect(1, 2 * (zs - 1), ready.at[1])
+        collect(1, LOCAL * (zs - 1), ready.at[1])
 
     def cot_start(i):
         h, k = H[i], H[1 - i]
@@ -300,8 +315,8 @@
             total = total + sums[k]
         inv_row[...] = lax.rsqrt(total / full_width + EPSILON)
 
-    def normed_rows():
-        @pl.loop(0, blocks)
+    def normed_rows(first, last):
+        @pl.loop(first * blocks // 2, last * blocks // 2)
         def _(b):
             rows = rows_of(b)
             column = column_of(inv_row[pl.ds(b, 1), :])
@@ -369,42 +384,39 @@
             total = total + (near[0, H[h]].astype(F32) + near[1, H[h]].astype(F32))
             keys_ref[H[h], :] = (total * inv_col[H[h], :]).astype(BF16)
 
-    def weight_grad_side(x_side):
-        @pl.loop(0, 2)
+    def weight_grad(first, last):
+        @pl.loop(first, last)
         def _(k):
-            p = x_side * 2 + k
-            rhs = jnp.concatenate([cotg[2 * p], cotg[2 * p + 1]], axis=1)
-            cols = pl.ds(pl.multiple_of(p * 2 * LANES, LANES), 2 * LANES)
-            for h in range(2):
-                rows = slice(h * (feats // 2), (h + 1) * (feats // 2))
-                wgrad_ref[rows, cols] = jnp.dot(
-                    normed_t[rows, :], rhs, preferred_element_type=F32
-                ).astype(BF16)
-
-    def normed_grads(first, last):
-        step = 2 * LANES
-
-        steps = tokens_n // step
-
+            weight_grad_pair(x_hi * 2 + k, cotg, normed_t, wgrad_ref)
+
+    def project(x_side):
+        @pl.loop(0, blocks)
+        def _(b):
+            rows = rows_of(b)
+            acc = jnp.zeros((LANES, LANES), F32)
+            for k in range(NY):
+                block = x_side * NY + k
+                acc = acc + cotg[block, rows, :].astype(F32) * parts[block, rows, :].astype(F32)
+            half_proj[x_side, pl.ds(b, 1), :] = lane_sum_row(acc)
+
+    step = 2 * LANES
+    steps = tokens_n // step
+
+    def cot_times_weight(x_side, rows):
+        lhs = jnp.concatenate([cotg[x_side * NY + k, rows, :] for k in range(NY)], axis=1)
+        cols = pl.ds(pl.multiple_of(x_side * NY * LANES, LANES), NY * LANES)
+        return lax.dot_general(
+            lhs, wt[:, cols], (((1,), (1,)), ((), ())), preferred_element_type=F32
+        )
+
+    def normed_grads_own(first, last):
         @pl.loop(first * steps // 4, last * steps // 4)
         def _(m):
             rows = pl.ds(pl.multiple_of(m * step, step), step)
-            lhs = jnp.concatenate([cotg[k, rows, :] for k in range(GROUP)], axis=1)
-            d = lax.dot_general(
-                lhs, wt[...], (((1,), (1,)), ((), ())), preferred_element_type=F32
-            )
-            d = d * gain[...]
-            dscaled[rows, :] = d
-            acc = jnp.zeros((step, LANES), F32)
-            for j in range(fblocks):
-                cols = slice(j * LANES, (j + 1) * LANES)
-                acc = acc + d[:, cols] * tok[rows, cols].astype(F32)
-            for k in range(step // LANES):
-                projs[t, pl.ds(m * (step // LANES) + k, 1), :] = lane_sum_row(
-                    acc[k * LANES : (k + 1) * LANES]
-                )
+            dpart[rows, :] = cot_times_weight(x_hi, rows)
 
     def proj_send():
+        projs[t] = half_proj[0] + half_proj[1]
         for d in range(1, GROUP):
             send(("proj", d), projs.at[t], projs.at[t], (r, (t + d) % GROUP))
 
@@ -418,16 +430,19 @@
         rowproj_ref[...] = projected * math.sqrt(full_width)
         other_row[...] = projected * inv_row[...] * inv_row[...]
 
-    def token_grads():
-        @pl.loop(0, blocks)
-        def _(b):
-            rows = rows_of(b)
+    def token_grads(first, last):
+        @pl.loop(first * steps // 4, last * steps // 4)
+        def _(m):
+            rows = pl.ds(pl.multiple_of(m * step, step), step)
+            d = dpart[rows, :] + cot_times_weight(1 - x_hi, rows)
             column = inv_col[rows, :]
-            other = column_of(other_row[pl.ds(b, 1), :])
+            other = jnp.concatenate(
+                [column_of(other_row[pl.ds(2 * m + k, 1), :]) for k in range(2)], axis=0
+            )
             for j in range(fblocks):
                 cols = slice(j * LANES, (j + 1) * LANES)
                 tgrad_ref[rows, cols] = (
-                    column * dscaled[rows, cols] - tok[rows, cols].astype(F32) * other
+                    column * (d[:, cols] * gain[:, cols]) - tok[rows, cols].astype(F32) * other
                 ).astype(BF16)
 
     def quantize(first, last):
@@ -451,7 +466,6 @@
     share_rows = qsend.shape[2]
     cut = share_rows // 32 * 16
     pieces = (slice(0, share_rows - cut), slice(share_rows - cut, share_rows))
-    far_first = sorted(range(1, zs), key=lambda d: -min(d, zs - d))
 
     def delta_start(i):
         p = pieces[i]
@@ -487,40 +501,33 @@
         for k in range(1, zs):
             total = total + r2[k, p, :]
         upd[e, z, p, :] = quantized(total / (LOCAL * zs), block_ones()).astype(BF16)
+        mine = upd.at[e, z, p]
+        for d in (*far_first, 0):
+            send(("r3x", i, d), mine, mine, of_local((z + d) % zs, e_xlo))
         for d in far_first:
-            send(("r3", i, d), upd.at[e, z, p], upd.at[e, z, p], of_local((z + d) % zs, e))
-
-    def update_local(i):
+            send(("r3", i, d), mine, mine, of_local((z + d) % zs, e))
+
+    def update_core(i):
         p = pieces[i]
+        for d in range(zs):
+            arrive(("r3x", i, d), upd.at[e_xlo, (z + zs - d) % zs, p])
         for d in range(1, zs):
             arrive(("r3", i, d), upd.at[e, (z + zs - d) % zs, p])
-        send(("r4x", i), upd.at[e, :, p], upd.at[e, :, p], of_local(z, e_xlo))
-        send(("r4c", i), upd.at[e, :, p], upd.at[e, :, p], of_local(z, e_core))
-
-    def update_core(i):
-        p = pieces[i]
-        arrive(("r4x", i), upd.at[e_xlo, :, p])
-        send(("r4xc", i), upd.at[e_xlo, :, p], upd.at[e_xlo, :, p], of_local(z, e_core))
+        both = upd.at[pl.ds(core * 2, 2), :, p]
+        send(("r4", i), both, both, of_local(z, e_core))
 
     def update_end():
         for i, p in enumerate(pieces):
-            arrive(("r4c", i), upd.at[e_core, :, p])
-            arrive(("r4xc", i), upd.at[e_diag, :, p])
-
-        @pl.loop(0, LOCAL * zs)
-        def _(s):
-            value = upd[s % LOCAL, s // LOCAL].astype(F32)
-            for k in range(width):
-                cols = pl.ds(pl.multiple_of(s * share + k * LANES, LANES), LANES)
-                update_ref[:, cols] = value[k * frag : (k + 1) * frag, :]
-
+            arrive(("r4", i), upd.at[pl.ds((1 - core) * 2, 2), :, p])
+
+    greet()
     load()
-    greet()
+    meet()
+    cot_start(0)
+    greet_z()
+    cot_start(1)
     quantize(0, 4)
-    meet()
     delta_start(0)
-    cot_start(0)
-    cot_start(1)
     delta_start(1)
     sum_squares()
     weight_ready()
@@ -530,42 +537,43 @@
     cot_onward(0)
     cot_onward(1)
     cot_far_start(0)
+    key_parts(x_hi)
     delta_sum(0)
     meet_z()
     delta_z(0)
     key_cross(0, 0)
     key_cross(0, 1)
+    cot_far_start(1)
     key_far_start(1)
     delta_sum(1)
     delta_z(1)
     sum_squares_end()
-    normed_rows()
-    key_parts(x_hi)
-    cot_far_start(1)
-    cot_own_end()
+    normed_rows(0, 2)
     key_two_away(0)
     key_two_away(1)
+    cot_own_end()
+    project(x_hi)
+    cot_far_onward(0)
+    cot_far_onward(1)
     delta_average(0)
+    key_own_start()
     key_cross(1, 0)
-    cot_far_onward(0)
     key_cross(1, 1)
-    cot_far_onward(1)
     delta_average(1)
     key_merge(0)
     key_merge(1)
-    key_own_start()
-    weight_grad_side(x_hi)
-    update_local(0)
+    weight_grad(0, 1)
     cot_far_end()
-    normed_grads(0, 4)
+    project(1 - x_hi)
     proj_send()
-    update_local(1)
-    weight_grad_side(1 - x_hi)
+    weight_grad(1, 2)
+    normed_grads_own(0, 4)
+    proj_end()
     update_core(0)
+    token_grads(0, 2)
     update_core(1)
+    token_grads(2, 4)
     key_end()
-    proj_end()
-    token_grads()
     update_end()
 
     for copy in pending:
@@ -577,7 +585,9 @@
     tgrad_ref,
     rowproj_ref,
     wgrad_ref,
-    update_ref,
+    upd_ref,
+    cotg_ref,
+    normed_t_ref,
     params_ref,
     momentum_ref,
     keys_hbm,
@@ -586,39 +596,53 @@
     wgrad_hbm,
     params_hbm,
     momentum_hbm,
+    wgrad_far,
     new_params,
     new_momentum,
     sem,
 ):
-    moves = [
-        (wgrad_ref, wgrad_hbm),
-        (tgrad_ref, tgrad_hbm),
-        (keys_ref, keys_hbm),
-        (rowproj_ref, rowproj_hbm),
-    ]
-    copies = [pltpu.make_async_copy(a, b, sem.at[i]) for i, (a, b) in enumerate(moves)]
-    for copy in copies:
+    x_hi = lax.axis_index("tensor") // NY
+    heads = wgrad_ref.shape[1]
+    own = pl.ds(pl.multiple_of(x_hi * (heads // 2), LANES), heads // 2)
+    copies = []
+
+    def write(src, dst):
+        copy = pltpu.make_async_copy(src, dst, sem.at[len(copies)])
         copy.start()
+        copies.append(copy)
+
+    write(tgrad_ref, tgrad_hbm)
+    write(wgrad_ref.at[:, own], wgrad_hbm.at[:, own])
+    write(keys_ref, keys_hbm)
+    write(rowproj_ref, rowproj_hbm)
+
     rows, columns = new_params.shape
-    parts = 4
-    step = columns // parts
-    for k in range(parts):
-        cols = pl.ds(k * step, step)
-
-        @pl.loop(0, rows // 8)
-        def _(b):
-            at = (pl.ds(pl.multiple_of(b * 8, 8), 8), cols)
-            update = update_ref[at]
-            moved = OUTER_MOMENTUM * momentum_ref[at] + update
-            new_momentum[at] = moved
-            new_params[at] = params_ref[at] - OUTER_RATE * (update + OUTER_MOMENTUM * moved)
-
-        for j, (a, b) in enumerate(((new_params, params_hbm), (new_momentum, momentum_hbm))):
-            copy = pltpu.make_async_copy(
-                a.at[:, cols], b.at[:, cols], sem.at[len(moves) + 2 * k + j]
-            )
-            copy.start()
-            copies.append(copy)
+    zs = upd_ref.shape[1]
+    share = columns // (LOCAL * zs)
+    groups = 4 if zs % 4 == 0 else 1
+    for g in range(groups):
+
+        @pl.loop(g * LOCAL * zs // groups, (g + 1) * LOCAL * zs // groups)
+        def _(s):
+            update = upd_ref[s % LOCAL, s // LOCAL].astype(F32)
+            for k in range(share // LANES):
+                cols = pl.ds(pl.multiple_of(s * share + k * LANES, LANES), LANES)
+                piece = update[k * rows : (k + 1) * rows, :]
+                moved = OUTER_MOMENTUM * momentum_ref[:, cols] + piece
+                new_momentum[:, cols] = moved
+                new_params[:, cols] = params_ref[:, cols] - OUTER_RATE * (
+                    piece + OUTER_MOMENTUM * moved
+                )
+
+        cols = pl.ds(g * (columns // groups), columns // groups)
+        write(new_params.at[:, cols], params_hbm.at[:, cols])
+        write(new_momentum.at[:, cols], momentum_hbm.at[:, cols])
+
+    for k in range(2):
+        pair = (1 - x_hi) * 2 + k
+        weight_grad_pair(pair, cotg_ref, normed_t_ref, wgrad_far)
+        cols = pl.ds(pl.multiple_of(pair * 2 * LANES, LANES), 2 * LANES)
+        write(wgrad_far.at[:, cols], wgrad_hbm.at[:, cols])
     for copy in copies:
         copy.wait()
 
@@ -637,25 +661,25 @@
     vmem = pl.BlockSpec(memory_space=pltpu.VMEM)
     blocks = tok_n // LANES
     operands = (tokens, norm_gain.reshape(1, feats), key_weight, key_cotangent, local_delta[0])
-    keys, tgrad, rowproj, wgrad, update = pl.pallas_call(
+    results = pl.pallas_call(
         functools.partial(kernel, full_width),
         out_shape=(
             jax.ShapeDtypeStruct((tok_n, kb), BF16),
             jax.ShapeDtypeStruct((tok_n, feats), BF16),
             jax.ShapeDtypeStruct((blocks, LANES), F32),
             jax.ShapeDtypeStruct((feats, heads), BF16),
-            jax.ShapeDtypeStruct((frag, row_width), F32),
+            jax.ShapeDtypeStruct((LOCAL, zs, share_rows, LANES), BF16),
+            jax.ShapeDtypeStruct((GROUP, tok_n, kb), BF16),
+            jax.ShapeDtypeStruct((feats, tok_n), BF16),
         ),
         in_specs=[hbm] * 5,
-        out_specs=(vmem,) * 5,
+        out_specs=(vmem,) * 7,
         scratch_shapes=[
             pltpu.VMEM((tok_n, feats), BF16),
             pltpu.VMEM((1, feats), F32),
             pltpu.VMEM(local_delta.shape[1:], BF16),
             pltpu.VMEM((feats, heads), BF16),
             pltpu.VMEM((tok_n, feats), BF16),
-            pltpu.VMEM((feats, tok_n), BF16),
-            pltpu.VMEM((GROUP, tok_n, kb), BF16),
             pltpu.VMEM((GROUP, tok_n, kb), BF16),
             pltpu.VMEM((tok_n, feats), F32),
             pltpu.VMEM((tok_n, LANES), F32),
@@ -663,6 +687,7 @@
             pltpu.VMEM((blocks, LANES), F32),
             pltpu.VMEM((GROUP, blocks, LANES), F32),
             pltpu.VMEM((GROUP, blocks, LANES), F32),
+            pltpu.VMEM((2, blocks, LANES), F32),
             pltpu.VMEM((2, 2, half, kb), BF16),
             pltpu.VMEM((2, 2, half, kb), BF16),
             pltpu.VMEM((2, 2, half, kb), BF16),
@@ -674,14 +699,13 @@
             pltpu.VMEM((LOCAL, zs, share_rows, LANES), BF16),
             pltpu.VMEM((zs, share_rows, LANES), F32),
             pltpu.VMEM((zs, share_rows, LANES), F32),
-            pltpu.VMEM((LOCAL, zs, share_rows, LANES), BF16),
             pltpu.SemaphoreType.REGULAR((2,)),
             pltpu.SemaphoreType.DMA((N_REMOTE,)),
             pltpu.SemaphoreType.DMA((N_REMOTE,)),
             pltpu.SemaphoreType.DMA((N_LOCAL,)),
         ],
         compiler_params=pltpu.CompilerParams(
-            collective_id=0, has_side_effects=True, vmem_limit_bytes=44 * 1024 * 1024
+            collective_id=0, has_side_effects=True, vmem_limit_bytes=36 * 1024 * 1024
         ),
         cost_estimate=pl.CostEstimate(
             flops=6 * tok_n * feats * heads, bytes_accessed=16 * 1024 * 1024, transcendentals=0
@@ -697,18 +721,19 @@
             jax.ShapeDtypeStruct((frag, row_width), F32),
             jax.ShapeDtypeStruct((frag, row_width), F32),
         ),
-        in_specs=[vmem] * 7,
+        in_specs=[vmem] * 9,
         out_specs=(hbm,) * 6,
         scratch_shapes=[
+            pltpu.VMEM((feats, heads), BF16),
             pltpu.VMEM((frag, row_width), F32),
             pltpu.VMEM((frag, row_width), F32),
-            pltpu.SemaphoreType.DMA((12,)),
+            pltpu.SemaphoreType.DMA((16,)),
         ],
         compiler_params=pltpu.CompilerParams(vmem_limit_bytes=16 * 1024 * 1024),
         cost_estimate=pl.CostEstimate(
             flops=8 * frag * row_width, bytes_accessed=8 * 1024 * 1024, transcendentals=0
         ),
-    )(keys, tgrad, rowproj, wgrad, update, outer_params, momentum)
+    )(*results, outer_params, momentum)
     return (keys, tgrad, rowproj.reshape(tok_n), wgrad[None], new_params, new_momentum)
 
 

time: 54.4 us -> 51.6 us (0.949)
  Pallas kernels: 53.6 us -> 50.8 us
    pallas_call x1, Pallas kernels: 50.6 us -> 47.8 us  [per_device(): pl.pallas_call(functools.partial(kernel, full_width), out_shape=(jax.Shap...]
where the time goes in v3:
time: 51.6 us; the launch traced here: 51.5 us
  Pallas kernels  50.8 us (98%)
  between operations  0.67 us (1%)
    pallas_call x1, Pallas kernels, per_device(): pl.pallas_call(functools.partial(kernel, full_width), out_shape=(jax.Shap...  47.8 us
    pallas_call x1, Pallas kernels, per_device(): pl.pallas_call(finish_kernel, out_shape=(jax.ShapeDtypeStruct((tok_n, kb)...  3.04 us

profile of v3, /device:TPU:1, one launch (start us, length us, event | category | flops | bytes accessed | tf_op | source)
XLA Modules:
  0.0 51.5 jit_solution(7820020190536967269)
XLA Ops:
  0.6 0.0 copy-start
  0.6 0.0 copy-start.1
  0.7 47.8 %shard_map.118 = (bf16[1024,128]{1,0:T(8,128)(2,1)S(1)}, bf16[1024,1024]{1,0:T(8,128)(2,1)S(1)}, f32[8,128]{1,0:T(8,128)S(1)}, bf16[1024,1024]{1,0:T(8,128)(2,1)...) custom-call(bf16[1024,1024]{1,0:T(8,128)(2,1)} %tok_hbm.1, ...), custom_call_target="tpu_custom_call" | custom-call | flops 6442450944 | bytes 16777216 | tf_op jit(solution)/shard_map/pallas_call | solution.py:664
  48.4 0.0 copy-done
  48.4 0.0 copy-done.1
  48.4 3.0 %shard_map.119 = (bf16[1024,128]{1,0:T(8,128)(2,1)}, bf16[1024,1024]{1,0:T(8,128)(2,1)}, f32[8,128]{1,0:T(8,128)}, bf16[1024,1024]{1,0:T(8,128)(2,1)}, f32[40,8192]{1,0:T(8,128)}, /*index=5*/f32[40,8192]{1,0:T(8,128)}) custom-call(bf16[1024,128]{1,0:T(8,128)(2,1)S(1)} %get-tuple-element.19.keys_ref, bf16[1024,1024]{1,0:T(8,128)(2,1)S(1)} %get-tuple-element.20.tgrad_ref, ...), custom_call_target="tpu_custom_call" | custom-call | flops 2621440 | bytes 8388608 | tf_op jit(solution)/shard_map/pallas_call | solution.py:714
Async XLA Ops:
  0.6 47.8 %copy-start = (f32[40,8192]{1,0:T(8,128)S(1)}, f32[40,8192]{1,0:T(8,128)}, u32[]{:S(2)}) copy-start(f32[40,8192]{1,0:T(8,128)} %params_ref.1) | copy-start | bytes 3932164
  0.6 47.8 %copy-start.1 = (f32[40,8192]{1,0:T(8,128)S(1)}, f32[40,8192]{1,0:T(8,128)}, u32[]{:S(2)}) copy-start(f32[40,8192]{1,0:T(8,128)} %momentum_ref.1) | copy-start | bytes 3932164

commit v4 on v3

--- a/solution.py
+++ b/solution.py
@@ -567,12 +567,13 @@
     project(1 - x_hi)
     proj_send()
     weight_grad(1, 2)
-    normed_grads_own(0, 4)
+    normed_grads_own(0, 2)
+    update_core(0)
+    normed_grads_own(2, 4)
     proj_end()
-    update_core(0)
-    token_grads(0, 2)
+    token_grads(0, 1)
     update_core(1)
-    token_grads(2, 4)
+    token_grads(1, 4)
     key_end()
     update_end()
 

time: 51.6 us -> 51 us (0.988)
  Pallas kernels: 50.8 us -> 50.2 us
    pallas_call x1, Pallas kernels: 47.8 us -> 47.2 us  [per_device(): pl.pallas_call(functools.partial(kernel, full_width), out_shape=(jax.Shap...]
where the time goes in v4:
time: 51 us; the launch traced here: 50.9 us
  Pallas kernels  50.2 us (98%)
  between operations  0.67 us (1%)
    pallas_call x1, Pallas kernels, per_device(): pl.pallas_call(functools.partial(kernel, full_width), out_shape=(jax.Shap...  47.2 us
    pallas_call x1, Pallas kernels, per_device(): pl.pallas_call(finish_kernel, out_shape=(jax.ShapeDtypeStruct((tok_n, kb)...  3.04 us

profile of v4, /device:TPU:1, one launch (start us, length us, event | category | flops | bytes accessed | tf_op | source)
XLA Modules:
  0.0 50.9 jit_solution(7935944881297769878)
XLA Ops:
  0.6 0.0 copy-start
  0.6 0.0 copy-start.1
  0.7 47.2 %shard_map.118 = (bf16[1024,128]{1,0:T(8,128)(2,1)S(1)}, bf16[1024,1024]{1,0:T(8,128)(2,1)S(1)}, f32[8,128]{1,0:T(8,128)S(1)}, bf16[1024,1024]{1,0:T(8,128)(2,1)...) custom-call(bf16[1024,1024]{1,0:T(8,128)(2,1)} %tok_hbm.1, ...), custom_call_target="tpu_custom_call" | custom-call | flops 6442450944 | bytes 16777216 | tf_op jit(solution)/shard_map/pallas_call | solution.py:665
  47.8 0.0 copy-done
  47.8 0.0 copy-done.1
  47.8 3.0 %shard_map.119 = (bf16[1024,128]{1,0:T(8,128)(2,1)}, bf16[1024,1024]{1,0:T(8,128)(2,1)}, f32[8,128]{1,0:T(8,128)}, bf16[1024,1024]{1,0:T(8,128)(2,1)}, f32[40,8192]{1,0:T(8,128)}, /*index=5*/f32[40,8192]{1,0:T(8,128)}) custom-call(bf16[1024,128]{1,0:T(8,128)(2,1)S(1)} %get-tuple-element.19.keys_ref, bf16[1024,1024]{1,0:T(8,128)(2,1)S(1)} %get-tuple-element.20.tgrad_ref, ...), custom_call_target="tpu_custom_call" | custom-call | flops 2621440 | bytes 8388608 | tf_op jit(solution)/shard_map/pallas_call | solution.py:715
Async XLA Ops:
  0.6 47.2 %copy-start = (f32[40,8192]{1,0:T(8,128)S(1)}, f32[40,8192]{1,0:T(8,128)}, u32[]{:S(2)}) copy-start(f32[40,8192]{1,0:T(8,128)} %params_ref.1) | copy-start | bytes 3932164
  0.6 47.2 %copy-start.1 = (f32[40,8192]{1,0:T(8,128)S(1)}, f32[40,8192]{1,0:T(8,128)}, u32[]{:S(2)}) copy-start(f32[40,8192]{1,0:T(8,128)} %momentum_ref.1) | copy-start | bytes 3932164
